TPU v7x, 256 devices: a whole 4x4x8 slice. The times are simulated.
256 devices in a mesh: seq: 32 (over y, x, core), exp: 8 (over z).
Axes of the slice: x: 4, y: 4, z: 8, core: 2. Of those that a mesh axis runs over, the one named last changes fastest.
Arguments:
- tokens: bfloat16 [4096, 4096], P('seq'), may hold values from -6 to 6
- cotangent: bfloat16 [4096, 4096], P('seq'), may hold values from -6 to 6
- expert_ids: int32 [4096, 2], P('seq'), may hold values from 0 to 15, all different within a row; in each aligned block of 128 rows (0 to 127, 128 to 255, ...) at most 24 rows name the same one
- ada_shift: float32 [4096], replicated, may hold values from -3 to 3
- ada_scale: float32 [4096], replicated, may hold values from -1.8 to 1.8
- ada_gate: float32 [4096], replicated, may hold values from 0.3 to 1.5
- router_weight: bfloat16 [4096, 16], replicated, may hold values from -0.09375 to 0.09375
- gate_blocks: bfloat16 [256, 4096, 128], P(('seq', 'exp')), may hold values from -0.09375 to 0.09375
- up_blocks: bfloat16 [256, 4096, 128], P(('seq', 'exp')), may hold values from -0.09375 to 0.09375
- down_blocks: bfloat16 [256, 128, 4096], P(('seq', 'exp')), may hold values from -0.125 to 0.125
Outputs:
- grad_input: float32 [4096, 4096], P('seq', 'exp')
- grad_router: float32 [4096, 16], P('exp')
- grad_gate: bfloat16 [256, 4096, 128], P(('seq', 'exp'))
- grad_up: bfloat16 [256, 4096, 128], P(('seq', 'exp'))
- grad_down: bfloat16 [256, 128, 4096], P(('seq', 'exp'))
Inputs may be any that keep to these rules, and one draw needn't show every extreme that they name: `expert_ids`: each row names two different experts; among the 128 rows of one index of seq no expert is named more than 24 times, a bound that some block reaches.
All inputs are finite; a program needn't handle non-finite values.
Results may differ from a plain program's by a relative error of at most 0.0082.
Values may be sent and summed in bfloat16 or wider, within the bound.
A program may use at most 128 MiB of HBM per device.

v0:
```python
import jax
import jax.numpy as jnp
from jax import lax
from jax.sharding import PartitionSpec as P

EXPERTS = 16
CAP = 24


EPSILON = 1e-06


def normalize(tokens, ada_shift, ada_scale):
    values = tokens.astype(jnp.float32)
    center = values - jnp.mean(values, axis=-1, keepdims=True)
    inv_std = lax.rsqrt(jnp.mean(center * center, axis=-1, keepdims=True) + EPSILON)
    normed = center * inv_std
    modulated = (normed * (1.0 + ada_scale) + ada_shift).astype(jnp.bfloat16)
    return (normed, inv_std, modulated)


def select_sum(onehot_b, values):
    high = values.astype(jnp.bfloat16)
    low = (values - high.astype(jnp.float32)).astype(jnp.bfloat16)
    dims = (((0,), (0,)), ((), ()))
    first = lax.dot_general(onehot_b, high, dims, preferred_element_type=jnp.float32)
    return first + lax.dot_general(onehot_b, low, dims, preferred_element_type=jnp.float32)


def expert_backward(rows_z, rows_dy, rows_share, gate_w, up_w, down_w):
    gate_pre = jnp.dot(rows_z, gate_w, preferred_element_type=jnp.float32)
    up_pre = jnp.dot(rows_z, up_w, preferred_element_type=jnp.float32)
    gate_sig = jax.nn.sigmoid(gate_pre)
    active = gate_pre * gate_sig
    hidden = active * up_pre
    back_hidden = lax.dot_general(
        rows_dy, down_w, (((1,), (1,)), ((), ())), preferred_element_type=jnp.float32
    )
    weight_terms = jnp.sum(hidden * back_hidden, axis=-1)
    weight_col = rows_share.astype(jnp.float32)[:, None]
    scaled = weight_col * back_hidden
    grad_up_pre = (scaled * active).astype(jnp.bfloat16)
    grad_gate_pre = (scaled * up_pre * gate_sig * (1.0 + gate_pre * (1.0 - gate_sig))).astype(
        jnp.bfloat16
    )
    grad_rows = lax.dot_general(
        grad_gate_pre, gate_w, (((1,), (1,)), ((), ())), preferred_element_type=jnp.float32
    )
    grad_rows = grad_rows + lax.dot_general(
        grad_up_pre, up_w, (((1,), (1,)), ((), ())), preferred_element_type=jnp.float32
    )
    grad_gate = lax.dot_general(
        rows_z, grad_gate_pre, (((0,), (0,)), ((), ())), preferred_element_type=jnp.float32
    )
    grad_up = lax.dot_general(
        rows_z, grad_up_pre, (((0,), (0,)), ((), ())), preferred_element_type=jnp.float32
    )
    hidden_b = hidden.astype(jnp.bfloat16)
    weighted_dy = (weight_col * rows_dy.astype(jnp.float32)).astype(jnp.bfloat16)
    grad_down = lax.dot_general(
        hidden_b, weighted_dy, (((0,), (0,)), ((), ())), preferred_element_type=jnp.float32
    )
    return (grad_rows, weight_terms, grad_gate, grad_up, grad_down)


def shards(
    tokens,
    cotangent,
    expert_ids,
    ada_shift,
    ada_scale,
    ada_gate,
    router_weight,
    gate_blocks,
    up_blocks,
    down_blocks,
):
    seq_count = lax.axis_size("seq")
    exp_count = lax.axis_size("exp")
    seq_index = lax.axis_index("seq")
    exp_index = lax.axis_index("exp")
    tok_rows = tokens.shape[0]
    model_width = tokens.shape[1]
    col_width = model_width // exp_count
    pieces = seq_count * exp_count // EXPERTS
    per_seq = max(1, exp_count // pieces)
    slot_count = seq_count * per_seq * CAP
    highest = lax.Precision.HIGHEST
    col_start = exp_index * col_width
    normed, inv_std, modulated = normalize(tokens, ada_shift, ada_scale)
    logits = jnp.dot(modulated, router_weight, preferred_element_type=jnp.float32)
    scores = jax.nn.sigmoid(logits)
    chosen = (expert_ids[:, :, None] == jnp.arange(EXPERTS, dtype=jnp.int32)[None, None, :]).astype(
        jnp.float32
    )
    picked = jnp.sum(chosen * scores[:, None, :], axis=-1)
    score_sum = jnp.sum(picked, axis=-1, keepdims=True)
    shares = picked / score_sum
    share_b = lax.optimization_barrier(shares.astype(jnp.bfloat16))
    expert_share = jnp.einsum("tke,tk->te", chosen, share_b.astype(jnp.float32))
    out_grad = (ada_gate * cotangent.astype(jnp.float32)).astype(jnp.bfloat16)
    flat_hits = chosen.reshape(tok_rows * 2, EXPERTS)
    before = jnp.cumsum(flat_hits, axis=0) - flat_hits
    slot_rank = jnp.sum(before * flat_hits, axis=-1).reshape(tok_rows, 2)
    rank_hit = (
        slot_rank[:, :, None] == jnp.arange(CAP, dtype=jnp.int32).astype(jnp.float32)[None, None, :]
    ).astype(jnp.float32)
    slot_table = jnp.einsum("tke,tkc->ect", chosen, rank_hit)
    dest_expert = (
        jnp.arange(seq_count, dtype=jnp.int32)[:, None] * exp_count // pieces
        + jnp.arange(per_seq, dtype=jnp.int32)[None, :]
    )
    dest_pick = (
        dest_expert.reshape(-1)[:, None] == jnp.arange(EXPERTS, dtype=jnp.int32)[None, :]
    ).astype(jnp.float32)
    dispatch = jnp.dot(dest_pick, slot_table.reshape(EXPERTS, CAP * tok_rows)).reshape(
        slot_count, tok_rows
    )
    slot_pick = jnp.repeat(dest_pick, CAP, axis=0)
    dispatch_b = dispatch.astype(jnp.bfloat16)
    slot_share = jnp.sum(jnp.dot(dispatch, expert_share) * slot_pick, axis=-1).astype(jnp.bfloat16)
    send_z = jnp.dot(dispatch_b, modulated, preferred_element_type=jnp.float32).astype(jnp.bfloat16)
    send_dy = jnp.dot(dispatch_b, out_grad, preferred_element_type=jnp.float32).astype(jnp.bfloat16)
    recv_z, recv_dy, recv_share = (
        lax.all_to_all(
            send_z.reshape(seq_count, per_seq * CAP, model_width),
            "seq",
            split_axis=0,
            concat_axis=0,
            tiled=True,
        ),
        lax.all_to_all(
            send_dy.reshape(seq_count, per_seq * CAP, model_width),
            "seq",
            split_axis=0,
            concat_axis=0,
            tiled=True,
        ),
        lax.all_to_all(
            slot_share.reshape(seq_count, per_seq * CAP),
            "seq",
            split_axis=0,
            concat_axis=0,
            tiled=True,
        ),
    )
    my_expert = (seq_index * exp_count + exp_index) // pieces
    my_slot = my_expert - seq_index * exp_count // pieces
    slot_start = my_slot * CAP
    rows_z = recv_z.reshape(seq_count * CAP, model_width)
    rows_dy = recv_dy.reshape(seq_count * CAP, model_width)
    rows_share = recv_share.reshape(seq_count * CAP)
    grad_rows, weight_terms, grad_gate, grad_up, grad_down = expert_backward(
        rows_z, rows_dy, rows_share, gate_blocks[0], up_blocks[0], down_blocks[0]
    )
    slot_mask = (jnp.arange(per_seq, dtype=jnp.int32) == my_slot).astype(jnp.float32)
    placed = (
        grad_rows.reshape(seq_count, 1, CAP, model_width) * slot_mask[None, :, None, None]
    ).reshape(seq_count, per_seq * CAP, model_width)
    placed_terms = (weight_terms.reshape(seq_count, 1, CAP) * slot_mask[None, :, None]).reshape(
        seq_count, per_seq * CAP
    )
    back_rows, back_terms = (
        lax.all_to_all(placed, "seq", split_axis=0, concat_axis=0, tiled=True),
        lax.all_to_all(placed_terms, "seq", split_axis=0, concat_axis=0, tiled=True),
    )
    token_grad = select_sum(dispatch_b, back_rows.reshape(slot_count, model_width))
    expert_grad = lax.psum_scatter(token_grad, "exp", scatter_dimension=1, tiled=True)
    term_part = select_sum(dispatch_b, back_terms.reshape(slot_count)[:, None] * slot_pick)
    weight_grad = lax.psum(term_part, "exp")
    choice_grad = jnp.sum(chosen * weight_grad[:, None, :], axis=-1)
    mean_grad = jnp.sum(shares * choice_grad, axis=-1, keepdims=True)
    pick_grad = (choice_grad - mean_grad) / score_sum * picked * (1.0 - picked)
    logit_grad = jnp.sum(chosen * pick_grad[:, :, None], axis=1)
    router_cols = lax.dynamic_slice_in_dim(router_weight, col_start, col_width, 0).astype(
        jnp.float32
    )
    modulated_cols = lax.dynamic_slice_in_dim(modulated, col_start, col_width, 1).astype(
        jnp.float32
    )
    mod_grad = expert_grad + lax.dot_general(
        logit_grad, router_cols, (((1,), (1,)), ((), ())), precision=highest
    )
    router_part = lax.dot_general(
        modulated_cols, logit_grad, (((0,), (0,)), ((), ())), precision=highest
    )
    grad_router = lax.psum(router_part, "seq")
    scale_cols = lax.dynamic_slice_in_dim(ada_scale, col_start, col_width, 0)
    normed_cols = lax.dynamic_slice_in_dim(normed, col_start, col_width, 1)
    norm_grad = mod_grad * (1.0 + scale_cols)
    grad_total, grad_cross = lax.psum(
        (jnp.sum(norm_grad, axis=-1), jnp.sum(norm_grad * normed_cols, axis=-1)), "exp"
    )
    grad_input = inv_std * (
        norm_grad
        - grad_total[:, None] / model_width
        - normed_cols * (grad_cross[:, None] / model_width)
    )
    return (
        grad_input,
        grad_router,
        grad_gate[None].astype(jnp.bfloat16),
        grad_up[None].astype(jnp.bfloat16),
        grad_down[None].astype(jnp.bfloat16),
    )


def solution(mesh):
    in_specs = (
        P("seq", None),
        P("seq", None),
        P("seq", None),
        P(),
        P(),
        P(),
        P(),
        P(("seq", "exp"), None, None),
        P(("seq", "exp"), None, None),
        P(("seq", "exp"), None, None),
    )
    out_specs = (
        P("seq", "exp"),
        P("exp", None),
        P(("seq", "exp"), None, None),
        P(("seq", "exp"), None, None),
        P(("seq", "exp"), None, None),
    )
    return jax.shard_map(shards, mesh=mesh, in_specs=in_specs, out_specs=out_specs, check_vma=False)
```

profile of v0, /device:TPU:32, one launch (start us, length us, event | category | flops | bytes accessed | tf_op | source)
XLA Modules:
  0.0 597.2 jit_solution(2577082679719525825)
XLA Ops:
  15.6 2.6 fusion.6
  18.2 4.4 convolution_convert_fusion
  22.6 7.6 %all-to-all-start.2 = ((bf16[32,24,4096]{2,1,0:T(8,128)(2,1)}), bf16[32,24,4096]{2,1,0:T(8,128)(2,1)}, u32[]{:S(2)}, u32[]{:S(2)}) async-start(bf16[32,24,4096]{2,1,0:T(8,128)(2,1)} %bitcast.95), calls=%async_computation.2 | async-start | bytes 12582912 | tf_op jit(solution)/shard_map/all_to_all | solution.py:125
  30.2 4.5 convolution_convert_fusion.1
  34.6 73.4 %all-to-all-done.2 = bf16[32,24,4096]{2,1,0:T(8,128)(2,1)} async-done(((bf16[32,24,4096]{2,1,0:T(8,128)(2,1)}), bf16[32,24,4096]{2,1,0:T(8,128)(2,1)}, u32[]{:S(2)}, u32[]{:S(2)}) %all-to-all-start.2) | async-done | bytes 6291488 | tf_op jit(solution)/shard_map/all_to_all | solution.py:125
  108.0 5.2 all-to-all-start.1
  113.7 5.9 fusion.16
  119.6 5.7 fusion.19
  125.3 65.7 %all-to-all-done.1 = bf16[32,24,4096]{2,1,0:T(8,128)(2,1)} async-done(((bf16[32,24,4096]{2,1,0:T(8,128)(2,1)}), bf16[32,24,4096]{2,1,0:T(8,128)(2,1)}, u32[]{:S(2)}, u32[]{:S(2)}) %all-to-all-start.1) | async-done | bytes 6291488 | tf_op jit(solution)/shard_map/all_to_all | solution.py:132
  191.0 6.2 %multiply_reduce_fusion = (f32[768]{0:T(1024)S(1)}, f32[768,128]{0,1:T(8,128)}) fusion(f32[768,128]{0,1:T(8,128)} %fusion.19, f32[768,128]{0,1:T(8,128)} %fusion.16, bf16[768,4096]{1,0:T(8,128)(2,1)} %bitcast.6, bf16[1,128,4096]{2,1,0:T(8,128)(2,1)} %param.19), kind=kOutput, calls=%fused_computation.41 | convolution fusion | flops 805993728 | bytes 8522752 | tf_op jit(solution)/shard_map/dot_general | solution.py:36
  197.9 4.5 all-to-all-start.4
  205.3 4.3 all-to-all-done.4
  215.4 18.1 %psum.28 = f32[128,16]{0,1:T(8,128)S(1)} all-reduce(f32[128,16]{0,1:T(8,128)S(1)} %convolution_add_fusion.2), channel_id=1, replica_groups=mesh['seq'=32,'exp'=8] {'exp'}, use_global_device_ids=true, to_apply=%region_10.11 | all-reduce | flops 2048 | bytes 16384 | tf_op jit(solution)/shard_map/psum | solution.py:170
  233.6 2.6 select_reduce_fusion
  239.4 10.8 %all_to_all.27 = bf16[32,1,24]{2,1,0:T(2,128)(2,1)S(1)} all-to-all(bf16[32,1,24]{2,1,0:T(2,128)(2,1)S(1)} %convert_element_type.216), channel_id=1, replica_groups=mesh['seq'=32,'exp'=8] {'seq'}, dimensions={0} | all-to-all | bytes 3072 | tf_op jit(solution)/shard_map/all_to_all | solution.py:139
  255.3 144.7 %all_to_all.28 = f32[32,24,4096]{2,1,0:T(8,128)} all-to-all(f32[32,24,4096]{2,1,0:T(8,128)S(1)} %bitcast.91), channel_id=1, replica_groups=mesh['seq'=32,'exp'=8] {'seq'}, dimensions={0} | all-to-all | bytes 25165824 | tf_op jit(solution)/shard_map/all_to_all | solution.py:164
  400.1 16.5 %subtract_convert_fusion = (bf16[32,24,4096]{2,1,0:T(8,128)(2,1)}, bf16[32,24,4096]{2,1,0:T(8,128)(2,1)}) fusion(f32[32,24,4096]{2,1,0:T(8,128)} %all_to_all.28), kind=kLoop, calls=%fused_computation.1 | loop fusion | flops 12582912 | bytes 25165824 | tf_op jit(solution)/shard_map/convert_element_type | solution.py:24
  416.6 3.9 fusion.53
  421.2 2.4 convolution_add_fusion
  425.1 129.0 %psum.31 = f32[512,16]{0,1:T(8,128)} all-reduce(f32[512,16]{0,1:T(8,128)S(1)} %fusion.32), channel_id=1, replica_groups=mesh['seq'=32,'exp'=8] {'seq'}, use_global_device_ids=true, to_apply=%region_18.19 | all-reduce | flops 8192 | bytes 65536 | tf_op jit(solution)/shard_map/psum | solution.py:187
  554.1 5.7 fusion.4
  559.8 5.7 fusion.3
  565.5 5.2 fusion.5
  572.1 16.4 %all-reduce = (f32[128]{0:T(128)S(1)}, f32[128]{0:T(128)S(1)}) all-reduce(f32[128]{0:T(128)S(1)} %get-tuple-element.6, f32[128]{0:T(128)S(1)} %get-tuple-element.5), channel_id=1, replica_groups=mesh['seq'=32,'exp'=8] {'exp'}, use_global_device_ids=true, to_apply=%region_17.18 | all-reduce | flops 256 | bytes 2048 | tf_op jit(solution)/shard_map/psum | solution.py:191
  (104 shorter events, 31.6 us)
Async XLA Ops:
  7.2 106.5 %copy-start = (bf16[1,4096,128]{2,1,0:T(8,128)(2,1)S(1)}, bf16[1,4096,128]{2,1,0:T(8,128)(2,1)}, u32[]{:S(2)}) copy-start(bf16[1,4096,128]{2,1,0:T(8,128)(2,1)} %param.17) | copy-start | bytes 3145732
  7.2 8.4 %copy-start.3 = (bf16[128,4096]{1,0:T(8,128)(2,1)S(1)}, bf16[128,4096]{1,0:T(8,128)(2,1)}, u32[]{:S(2)}) copy-start(bf16[128,4096]{1,0:T(8,128)(2,1)} %param.10) | copy-start | bytes 3145732
  7.2 8.0 %copy-start.20 = (s32[32]{0:T(128)}, s32[32]{0:T(128)S(1)}, u32[]{:S(2)}) copy-start(s32[32]{0:T(128)S(1)} %and_select_fusion) | copy-start | bytes 388
  8.2 7.3 %copy-start.12 = (s32[128,2]{1,0:T(8,128)}, s32[128,2]{1,0:T(8,128)S(1)}, u32[]{:S(2)}) copy-start(s32[128,2]{1,0:T(8,128)S(1)} %copy.44) | copy-start | bytes 3076
  22.6 7.6 %copy-start.15 = (bf16[128,4096]{1,0:T(8,128)(2,1)S(1)}, bf16[128,4096]{1,0:T(8,128)(2,1)}, u32[]{:S(2)}) copy-start(bf16[128,4096]{1,0:T(8,128)(2,1)} %param.11) | copy-start | bytes 3145732
  22.6 7.6 %copy-start.17 = (f32[4096]{0:T(1024)S(1)}, f32[4096]{0:T(1024)}, u32[]{:S(2)}) copy-start(f32[4096]{0:T(1024)} %param.15) | copy-start | bytes 49156
  22.6 85.4 %all-to-all-start.2 = ((bf16[32,24,4096]{2,1,0:T(8,128)(2,1)}), bf16[32,24,4096]{2,1,0:T(8,128)(2,1)}, u32[]{:S(2)}, u32[]{:S(2)}) async-start(bf16[32,24,4096]{2,1,0:T(8,128)(2,1)} %bitcast.95), calls=%async_computation.2 | async-start | bytes 12582912 | tf_op jit(solution)/shard_map/all_to_all | solution.py:125
  108.0 5.3 copy-start.16
  108.0 83.0 %all-to-all-start.1 = ((bf16[32,24,4096]{2,1,0:T(8,128)(2,1)}), bf16[32,24,4096]{2,1,0:T(8,128)(2,1)}, u32[]{:S(2)}, u32[]{:S(2)}) async-start(bf16[32,24,4096]{2,1,0:T(8,128)(2,1)} %bitcast.94), calls=%async_computation.1 | async-start | bytes 12582912 | tf_op jit(solution)/shard_map/all_to_all | solution.py:132
  113.7 5.9 copy-start.4
  125.3 77.2 %copy-start.21 = (s32[32]{0:T(128)S(1)}, s32[32]{0:T(128)}, u32[]{:S(2)}) copy-start(s32[32]{0:T(128)} %copy-done.20) | copy-start | bytes 388
  125.3 108.3 %copy-start.13 = (s32[128,2]{1,0:T(8,128)S(1)}, s32[128,2]{1,0:T(8,128)}, u32[]{:S(2)}) copy-start(s32[128,2]{1,0:T(8,128)} %copy-done.12) | copy-start | bytes 3076
  191.0 59.4 %copy-start.6 = (f32[768,128]{0,1:T(8,128)S(1)}, f32[768,128]{0,1:T(8,128)}, u32[]{:S(2)}) copy-start(f32[768,128]{0,1:T(8,128)} %fusion.16) | copy-start | bytes 1179652
  191.0 59.4 %copy-start.8 = (f32[768,128]{0,1:T(8,128)S(1)}, f32[768,128]{0,1:T(8,128)}, u32[]{:S(2)}) copy-start(f32[768,128]{0,1:T(8,128)} %fusion.19) | copy-start | bytes 1179652
  197.9 11.6 %all-to-all-start.4 = ((f32[32,1,24]{2,1,0:T(1,128)}), f32[32,1,24]{2,1,0:T(1,128)}, u32[]{:S(2)}, u32[]{:S(2)}) async-start(f32[32,1,24]{2,1,0:T(1,128)} %bitcast.15), calls=%async_computation.5 | async-start | bytes 32768 | tf_op jit(solution)/shard_map/all_to_all | solution.py:165
  202.5 368.3 %reduce-scatter.2.cloned.1.call-start = ((), (), s32[]{:S(2)}) async-start(), calls=%async_computation.6 | async-start | bytes 2359296 | tf_op jit(solution)/shard_map/reduce_scatter | solution.py:168
  416.6 4.6 copy-start.2
  421.2 3.2 copy-start.22
  421.2 3.4 copy-start.14
  423.6 136.2 %copy-start.11 = (bf16[768,128]{0,1:T(8,128)(2,1)S(1)}, bf16[768,128]{0,1:T(8,128)(2,1)}, u32[]{:S(2)}) copy-start(bf16[768,128]{0,1:T(8,128)(2,1)} %copy-done.10) | copy-start | bytes 589828
  554.1 11.4 %copy-start.7 = (f32[768,128]{0,1:T(8,128)S(1)}, f32[768,128]{0,1:T(8,128)}, u32[]{:S(2)}) copy-start(f32[768,128]{0,1:T(8,128)} %fusion.16) | copy-start | bytes 1179652
  554.1 11.4 %copy-start.9 = (f32[768,128]{0,1:T(8,128)S(1)}, f32[768,128]{0,1:T(8,128)}, u32[]{:S(2)}) copy-start(f32[768,128]{0,1:T(8,128)} %fusion.19) | copy-start | bytes 1179652
  559.8 30.5 %copy-start.1 = (bf16[1,4096,128]{2,1,0:T(8,128)(2,1)S(1)}, bf16[1,4096,128]{2,1,0:T(8,128)(2,1)}, u32[]{:S(2)}) copy-start(bf16[1,4096,128]{2,1,0:T(8,128)(2,1)} %param.17) | copy-start | bytes 3145732
  565.5 23.0 %copy-start.19 = (f32[128]{0:T(128)S(1)}, f32[128]{0:T(128)}, u32[]{:S(2)}) copy-start(f32[128]{0:T(128)} %add_rsqrt_fusion) | copy-start | bytes 1540
  (3 other events, 6.0 us)
Sparse Core Ops, SparseCore 0:
  423.7 41.2 reduce-scatter.1
where the time goes:
time: 598 us; the launch traced here: 597 us
  blocking collectives  319 us (53%)
  waiting for transfers between devices  143 us (24%)
  matrix products  59.6 us (10%)
  other arithmetic  33.2 us (6%)
  starting transfers between devices  17.3 us (3%)
  between operations  14.4 us (2%)
  local copies, waits for them, and re-layouts  10.3 us (2%)
    all_to_all x1, blocking collectives, shards(): lax.all_to_all(placed, 'seq', split_axis=0, concat_axis=0, tiled=True)  145 us
    psum x1, blocking collectives, shards(): grad_router = lax.psum(router_part, 'seq')  129 us
    all_to_all x1, waiting for transfers between devices, shards(): lax.all_to_all(send_z.reshape(seq_count, per_seq * CAP, model_width), 'se...  73.4 us
    all_to_all x1, waiting for transfers between devices, shards(): lax.all_to_all(send_dy.reshape(seq_count, per_seq * CAP, model_width), 's...  65.7 us
    psum x1, blocking collectives, shards(): weight_grad = lax.psum(term_part, 'exp')  18.1 us
    convert_element_type x2, other arithmetic, select_sum(): low = (values - high.astype(jnp.float32)).astype(jnp.bfloat16)  18 us
    psum x1, blocking collectives, shards(): lax.psum((jnp.sum(norm_grad, axis=-1), jnp.sum(norm_grad * normed_cols, a...  16.4 us
  transfers between devices with their start and end apart: 4, of which 3 were waited for; matrix products, arithmetic and copies ran while one was open for 6% of the time, Pallas kernels for 0%

commit v1 on v0

v1 whole, which is shorter than its diff:
```python
import functools
import math

import jax
import jax.numpy as jnp
from jax import lax
from jax.experimental import pallas as pl
from jax.experimental.pallas import tpu as pltpu
from jax.sharding import PartitionSpec as P

CAP = 24
EPSILON = 1e-06
MESH = pl.DeviceIdType.MESH
F32 = jnp.float32
BF16 = jnp.bfloat16
NT = (((1,), (1,)), ((), ()))
TN = (((0,), (0,)), ((), ()))


def dot(a, b, dims=(((1,), (0,)), ((), ()))):
    return lax.dot_general(a, b, dims, preferred_element_type=F32)


def expert_kernel(
    n,
    zn,
    send,
    gate,
    up,
    down,
    back_out,
    terms_out,
    gate_out,
    up_out,
    down_out,
    recv,
    w_gate,
    w_up,
    w_down,
    rows_z,
    rows_wdy,
    d_gu,
    hid,
    hr,
    g_acc,
    u_acc,
    r_acc,
    t_send,
    t_recv,
    b_send,
    b_recv,
    term_own,
    term_z,
    term_sum,
    term_b,
    gu_own,
    gu_send,
    gu_recv,
    dn_own,
    dn_send,
    dn_recv,
    w_local,
    w_ssem,
    w_rsem,
    d_ssem,
    d_rsem,
    t_ssem,
    t_rsem,
    b_ssem,
    b_rsem,
    tz_ssem,
    tz_rsem,
    tb_ssem,
    tb_rsem,
    g_ssem,
    g_rsem,
    h_ssem,
    h_rsem,
):
    slots = n * n
    width = rows_z.shape[1]
    group = n * CAP
    hidden = w_gate.shape[2]
    kb = 512
    nb = width // kb
    cols_z = width // zn
    half = cols_z // 2
    seq = lax.axis_index("seq")
    z = lax.axis_index("exp")
    core = lax.rem(seq, 2)
    chip = seq // 2
    cy, cx = chip // n, lax.rem(chip, n)

    def offset(slot):
        dy = lax.rem(slot, n)
        dx = lax.rem(dy + slot // n, n)
        return dy, dx

    def target(slot):
        dy, dx = offset(slot)
        return (2 * (lax.rem(cy + dy, n) * n + lax.rem(cx + dx, n)) + core, z)

    def source(slot):
        dy, dx = offset(slot)
        return (2 * (lax.rem(cy - dy + n, n) * n + lax.rem(cx - dx + n, n)) + core, z)

    def z_peer(step):
        return (seq, lax.rem(z + step, zn))

    sibling = (seq + 1 - 2 * core, z)

    def remote(src, dst, ssem, rsem, dev):
        return pltpu.make_async_remote_copy(
            src_ref=src, dst_ref=dst, send_sem=ssem, recv_sem=rsem, device_id=dev, device_id_type=MESH
        )

    def send_copy(slot):
        return remote(send.at[slot], recv.at[slot], d_ssem.at[slot], d_rsem.at[slot], target(slot))

    def t_copy(g, step):
        return remote(
            t_send.at[g, step], t_recv.at[g, step], t_ssem.at[g, step], t_rsem.at[g, step], z_peer(step)
        )

    def b_copy(slot):
        return remote(b_send.at[slot], b_recv.at[slot], b_ssem.at[slot], b_rsem.at[slot], source(slot))

    def tz_copy(step):
        return remote(term_own, term_z.at[step], tz_ssem.at[step], tz_rsem.at[step], z_peer(step))

    def tb_copy(slot):
        return remote(term_sum, term_b.at[slot], tb_ssem.at[slot], tb_rsem.at[slot], source(slot))

    def gu_copy(b):
        return remote(gu_send.at[b], gu_recv.at[b], g_ssem.at[b], g_rsem.at[b], sibling)

    def dn_copy(b):
        return remote(dn_send.at[b], dn_recv.at[b], h_ssem.at[b], h_rsem.at[b], sibling)

    weights = ((gate, w_gate), (up, w_up), (down, w_down))

    def w_copy(i):
        hbm, vmem = weights[i]
        return remote(hbm.at[0], vmem.at[1], w_ssem.at[i], w_rsem.at[i], sibling)

    def w_copy_local(i):
        hbm, vmem = weights[i]
        return pltpu.make_async_copy(hbm.at[0], vmem.at[0], w_local.at[i])

    def loop(lo, hi, body):
        def step(i, carry):
            body(i)
            return carry

        lax.fori_loop(lo, hi, step, 0)

    barrier = pltpu.get_barrier_semaphore()
    loop(
        1,
        slots,
        lambda k: pl.semaphore_signal(barrier, inc=1, device_id=target(k), device_id_type=MESH),
    )
    loop(
        1,
        zn,
        lambda j: pl.semaphore_signal(barrier, inc=1, device_id=z_peer(j), device_id_type=MESH),
    )
    pl.semaphore_signal(barrier, inc=1, device_id=sibling, device_id_type=MESH)
    own = pltpu.make_async_copy(send.at[0], recv.at[0], w_local.at[3])
    own.start()
    for i in range(3):
        w_copy_local(i).start()
    pl.semaphore_wait(barrier, slots + zn - 1)

    for i in range(3):
        w_copy(i).start()
    loop(1, slots, lambda k: send_copy(k).start())
    hr[...] = jnp.zeros_like(hr)
    own.wait()
    for i in range(3):
        w_copy_local(i).wait()
        w_copy(i).wait()

    def wait_group(g):
        def one(i):
            slot = g * n + i

            @pl.when(slot > 0)
            def _():
                send_copy(slot).wait_recv()

        loop(0, n, one)

    def reduce_group(g):
        loop(1, zn, lambda j: t_copy(g, j).wait_recv())
        for i in range(n):
            slot = g * n + i
            parts = []
            for lo in (0, half):
                part = t_recv[g, :, :, lo : lo + half].astype(F32)[:, i * CAP : (i + 1) * CAP, :]
                parts.append(jnp.sum(part, axis=0))
            packed = jnp.concatenate(parts, axis=0).astype(BF16)
            if i > 0:
                b_send[slot] = packed
                b_copy(slot).start()
            else:

                @pl.when(slot > 0)
                def _():
                    b_send[slot] = packed
                    b_copy(slot).start()

                @pl.when(slot == 0)
                def _():
                    b_recv[0] = packed

    def compute_group(g):
        wait_group(g)
        rows = pl.ds(pl.multiple_of(g * group, group), group)
        share = jnp.concatenate(
            [recv[g * n + i, :, width : width + 128].astype(F32)[CAP:, :1] for i in range(n)], axis=0
        )
        g_acc[...] = jnp.zeros_like(g_acc)
        u_acc[...] = jnp.zeros_like(u_acc)
        r_acc[...] = jnp.zeros_like(r_acc)

        def forward(b):
            cols = pl.ds(pl.multiple_of(b * kb, kb), kb)
            tiles = [recv[g * n + i, :, cols].astype(F32) for i in range(n)]
            zb = jnp.concatenate([t[:CAP] for t in tiles], axis=0).astype(BF16)
            dyf = jnp.concatenate([t[CAP:] for t in tiles], axis=0)
            rows_z[rows, cols] = zb
            rows_wdy[rows, cols] = (share * dyf).astype(BF16)
            g_acc[...] += dot(zb, jnp.concatenate([w_gate[0, cols, :], w_gate[1, cols, :]], axis=1))
            u_acc[...] += dot(zb, jnp.concatenate([w_up[0, cols, :], w_up[1, cols, :]], axis=1))
            wd = jnp.concatenate([w_down[0, :, cols], w_down[1, :, cols]], axis=0)
            r_acc[...] += dot(dyf.astype(BF16), wd, NT)

        loop(0, nb, forward)
        gv, uv, rv = g_acc[...], u_acc[...], r_acc[...]
        sig = jax.nn.sigmoid(gv)
        act = gv * sig
        hv = act * uv
        prod = hv * rv
        hr[rows, :] = prod[:, :hidden] + prod[:, hidden:]
        scaled = share * rv
        du = (scaled * act).astype(BF16)
        dg = (scaled * uv * sig * (1.0 + gv * (1.0 - sig))).astype(BF16)
        d_gu[rows, :] = jnp.concatenate(
            [dg[:, :hidden], du[:, :hidden], dg[:, hidden:], du[:, hidden:]], axis=1
        )
        hid[rows, :] = hv.astype(BF16)

        def backward(step):
            dest = lax.rem(z + step, zn)
            wrows = pl.ds(pl.multiple_of(dest * cols_z, cols_z), cols_z)
            wg = jnp.concatenate([w_gate[0, wrows, :], w_gate[1, wrows, :]], axis=1)
            wu = jnp.concatenate([w_up[0, wrows, :], w_up[1, wrows, :]], axis=1)
            part = (dot(dg, wg, NT) + dot(du, wu, NT)).astype(BF16)

            @pl.when(step > 0)
            def _():
                t_send[g, step] = part
                t_copy(g, step).start()

            @pl.when(step == 0)
            def _():
                t_recv[g, 0] = part

        loop(0, zn, lambda i: backward(zn - 1 - i))

    def group_step(g):
        compute_group(g)

        @pl.when(g > 0)
        def _():
            reduce_group(g - 1)

    loop(0, n, group_step)

    nt = hr.shape[0] // 128
    term_own[...] = jnp.zeros_like(term_own)
    for i in range(nt):
        tile = hr[128 * i : 128 * (i + 1), :]
        term_own[i : i + 1, :] = jnp.sum(tile.T, axis=0, keepdims=True)
    loop(1, zn, lambda j: tz_copy(j).start())

    def weight_grads(b):
        cols = pl.ds(pl.multiple_of(b * kb, kb), kb)
        gu = dot(rows_z[:, cols], d_gu[...], TN)
        gu_own[b] = gu[:, : 2 * hidden]
        gu_send[b] = gu[:, 2 * hidden :].astype(BF16)
        gu_copy(b).start()
        dn = dot(hid[...], rows_wdy[:, cols], TN)
        dn_own[b] = dn[:hidden]
        dn_send[b] = dn[hidden:].astype(BF16)
        dn_copy(b).start()

    loop(0, nb // 2, weight_grads)
    loop(1, zn, lambda j: tz_copy(j).wait_recv())
    total = term_own[...]
    for j in range(1, zn):
        total = total + term_z[j]
    term_sum[...] = total
    loop(1, slots, lambda k: tb_copy(k).start())
    loop(nb // 2, nb, weight_grads)
    reduce_group(n - 1)

    def finish(b):
        gu_copy(b).wait_recv()
        dn_copy(b).wait_recv()
        cols = pl.ds(pl.multiple_of(b * kb, kb), kb)
        gu = gu_own[b] + gu_recv[b].astype(F32)
        gate_out[0, cols, :] = gu[:, :hidden].astype(BF16)
        up_out[0, cols, :] = gu[:, hidden:].astype(BF16)
        down_out[0, :, cols] = (dn_own[b] + dn_recv[b].astype(F32)).astype(BF16)

    loop(0, nb, finish)

    loop(1, slots, lambda k: tb_copy(k).wait_recv())
    flat = lax.broadcasted_iota(jnp.int32, (8, 128), 0) * 128 + lax.broadcasted_iota(
        jnp.int32, (8, 128), 1
    )
    terms = jnp.where(flat < CAP, term_sum[...], 0.0)
    for k in range(1, slots):
        terms = jnp.where((flat >= k * CAP) & (flat < (k + 1) * CAP), term_b[k], terms)
    terms_out[...] = terms

    loop(1, slots, lambda k: b_copy(k).wait_recv())
    back_out[...] = b_recv[...]

    def drain_slot(k):
        send_copy(k).wait_send()
        b_copy(k).wait_send()
        tb_copy(k).wait_send()

    loop(1, slots, drain_slot)

    def drain_z(j):
        tz_copy(j).wait_send()
        loop(0, n, lambda g: t_copy(g, j).wait_send())

    loop(1, zn, drain_z)

    def drain_b(b):
        gu_copy(b).wait_send()
        dn_copy(b).wait_send()

    loop(0, nb, drain_b)


def run_experts(n, zn, send, gate, up, down):
    slots = n * n
    width, hidden = gate.shape[1], gate.shape[2]
    rows = slots * CAP
    cols_z = width // zn
    nb = width // 512
    nt = -(-rows // 128)
    dma = pltpu.SemaphoreType.DMA
    vm = pltpu.VMEM
    scratch = [
        vm(send.shape, BF16),
        vm((2, width, hidden), BF16),
        vm((2, width, hidden), BF16),
        vm((2, hidden, width), BF16),
        vm((rows, width), BF16),
        vm((rows, width), BF16),
        vm((rows, 4 * hidden), BF16),
        vm((rows, 2 * hidden), BF16),
        vm((nt * 128, hidden), F32),
        vm((n * CAP, 2 * hidden), F32),
        vm((n * CAP, 2 * hidden), F32),
        vm((n * CAP, 2 * hidden), F32),
        vm((n, zn, n * CAP, cols_z), BF16),
        vm((n, zn, n * CAP, cols_z), BF16),
        vm((slots, 2 * CAP, cols_z // 2), BF16),
        vm((slots, 2 * CAP, cols_z // 2), BF16),
        vm((8, 128), F32),
        vm((zn, 8, 128), F32),
        vm((8, 128), F32),
        vm((slots, 8, 128), F32),
        vm((nb, 512, 2 * hidden), F32),
        vm((nb, 512, 2 * hidden), BF16),
        vm((nb, 512, 2 * hidden), BF16),
        vm((nb, hidden, 512), F32),
        vm((nb, hidden, 512), BF16),
        vm((nb, hidden, 512), BF16),
        dma((4,)),
        dma((3,)),
        dma((3,)),
        dma((slots,)),
        dma((slots,)),
        dma((n, zn)),
        dma((n, zn)),
        dma((slots,)),
        dma((slots,)),
        dma((zn,)),
        dma((zn,)),
        dma((slots,)),
        dma((slots,)),
        dma((nb,)),
        dma((nb,)),
        dma((nb,)),
        dma((nb,)),
    ]
    any_spec = pl.BlockSpec(memory_space=pl.ANY)
    vm_spec = pl.BlockSpec(memory_space=pltpu.VMEM)
    return pl.pallas_call(
        functools.partial(expert_kernel, n, zn),
        out_shape=(
            jax.ShapeDtypeStruct((slots, 2 * CAP, cols_z // 2), BF16),
            jax.ShapeDtypeStruct((8, 128), F32),
            jax.ShapeDtypeStruct((1, width, hidden), BF16),
            jax.ShapeDtypeStruct((1, width, hidden), BF16),
            jax.ShapeDtypeStruct((1, hidden, width), BF16),
        ),
        in_specs=[any_spec] * 4,
        out_specs=(vm_spec,) * 5,
        scratch_shapes=scratch,
        compiler_params=pltpu.CompilerParams(
            collective_id=0, has_side_effects=True, vmem_limit_bytes=58 * 1024 * 1024
        ),
        cost_estimate=pl.CostEstimate(
            flops=16 * rows * width * 2 * hidden, bytes_accessed=16 * 1024 * 1024, transcendentals=0
        ),
    )(send, gate, up, down)


def shards(
    tokens,
    cotangent,
    expert_ids,
    ada_shift,
    ada_scale,
    ada_gate,
    router_weight,
    gate_blocks,
    up_blocks,
    down_blocks,
):
    zn = lax.axis_size("exp")
    experts = lax.axis_size("seq") // 2
    n = math.isqrt(experts)
    seq_index = lax.axis_index("seq")
    exp_index = lax.axis_index("exp")
    tok_rows, width = tokens.shape
    cols = width // zn
    slots = n * n
    highest = lax.Precision.HIGHEST
    col_start = exp_index * cols

    values = tokens.astype(F32)
    center = values - jnp.mean(values, axis=-1, keepdims=True)
    inv_std = lax.rsqrt(jnp.mean(center * center, axis=-1, keepdims=True) + EPSILON)
    normed = center * inv_std
    modulated = (normed * (1.0 + ada_scale) + ada_shift).astype(BF16)
    scores = jax.nn.sigmoid(dot(modulated, router_weight))
    expert_iota = jnp.arange(experts, dtype=jnp.int32)
    chosen = (expert_ids[:, :, None] == expert_iota[None, None, :]).astype(F32)
    picked = jnp.sum(chosen * scores[:, None, :], axis=-1)
    score_sum = jnp.sum(picked, axis=-1, keepdims=True)
    shares = picked / score_sum
    share_b = lax.optimization_barrier(shares.astype(BF16))
    out_grad = (ada_gate * cotangent.astype(F32)).astype(BF16)

    routed = jnp.sum(chosen, axis=1)
    tok_iota = jnp.arange(tok_rows, dtype=jnp.int32)
    earlier = (tok_iota[:, None] > tok_iota[None, :]).astype(BF16)
    rank_all = dot(earlier, routed.astype(BF16))
    rank = jnp.sum(chosen * rank_all[:, None, :], axis=-1).astype(jnp.int32)
    chip = seq_index // 2
    dy = lax.rem(expert_ids // n - chip // n + n, n)
    dx = lax.rem(lax.rem(expert_ids, n) - lax.rem(chip, n) + n, n)
    slot = (lax.rem(dx - dy + n, n) * n + dy) * CAP + rank
    slot_iota = jnp.arange(slots * CAP, dtype=jnp.int32)
    hit = slot[:, :, None] == slot_iota[None, None, :]
    place = jnp.any(hit, axis=1).astype(BF16)
    slot_share = jnp.sum(jnp.where(hit, share_b.astype(F32)[:, :, None], 0.0), axis=(0, 1))

    send_z = dot(place, modulated, TN).astype(BF16)
    send_dy = dot(place, out_grad, TN).astype(BF16)
    side = jnp.broadcast_to(slot_share.astype(BF16)[:, None], (slots * CAP, 128))
    send = jnp.concatenate(
        [
            jnp.concatenate([send_z, side], axis=1).reshape(slots, CAP, width + 128),
            jnp.concatenate([send_dy, side], axis=1).reshape(slots, CAP, width + 128),
        ],
        axis=1,
    )
    back, terms, grad_gate, grad_up, grad_down = run_experts(
        n, zn, send, gate_blocks, up_blocks, down_blocks
    )
    rows_back = (
        back.reshape(slots, 2, CAP, cols // 2).transpose(0, 2, 1, 3).reshape(slots * CAP, cols)
    )
    expert_grad = dot(place, rows_back)
    term_row = terms.reshape(-1)[: slots * CAP]
    choice_grad = jnp.sum(jnp.where(hit, term_row[None, None, :], 0.0), axis=-1)
    mean_grad = jnp.sum(shares * choice_grad, axis=-1, keepdims=True)
    pick_grad = (choice_grad - mean_grad) / score_sum * picked * (1.0 - picked)
    logit_grad = jnp.sum(chosen * pick_grad[:, :, None], axis=1)
    router_cols = lax.dynamic_slice_in_dim(router_weight, col_start, cols, 0).astype(F32)
    modulated_cols = lax.dynamic_slice_in_dim(modulated, col_start, cols, 1).astype(F32)
    mod_grad = expert_grad + lax.dot_general(logit_grad, router_cols, NT, precision=highest)
    router_part = lax.dot_general(modulated_cols, logit_grad, TN, precision=highest)
    grad_router = lax.psum(router_part, "seq")
    scale_cols = lax.dynamic_slice_in_dim(ada_scale, col_start, cols, 0)
    normed_cols = lax.dynamic_slice_in_dim(normed, col_start, cols, 1)
    norm_grad = mod_grad * (1.0 + scale_cols)
    grad_total, grad_cross = lax.psum(
        (jnp.sum(norm_grad, axis=-1), jnp.sum(norm_grad * normed_cols, axis=-1)), "exp"
    )
    grad_input = inv_std * (
        norm_grad - grad_total[:, None] / width - normed_cols * (grad_cross[:, None] / width)
    )
    return (grad_input, grad_router, grad_gate, grad_up, grad_down)


def solution(mesh):
    in_specs = (
        P("seq", None),
        P("seq", None),
        P("seq", None),
        P(),
        P(),
        P(),
        P(),
        P(("seq", "exp"), None, None),
        P(("seq", "exp"), None, None),
        P(("seq", "exp"), None, None),
    )
    out_specs = (
        P("seq", "exp"),
        P("exp", None),
        P(("seq", "exp"), None, None),
        P(("seq", "exp"), None, None),
        P(("seq", "exp"), None, None),
    )
    return jax.shard_map(shards, mesh=mesh, in_specs=in_specs, out_specs=out_specs, check_vma=False)
```

time: 598 us -> 304 us (0.51)
  blocking collectives: 319 us -> 142 us
  waiting for transfers between devices: 143 us -> 0 us
  Pallas kernels: 0 us -> 138 us
  matrix products: 59.6 us -> 4.18 us
  other arithmetic: 33.2 us -> 12.4 us
  starting transfers between devices: 17.3 us -> 0 us
  between operations: 14.4 us -> 0.88 us
    all_to_all x2 -> x0, blocking collectives: 156 us -> none  [the longest x1 145 us: shards(): lax.all_to_all(placed, 'seq', split_axis=0, concat_axis=0, tiled=True)]
    all_to_all x3 -> x0, waiting for transfers between devices: 143 us -> none  [the longest x1 73.4 us: shards(): lax.all_to_all(send_z.reshape(seq_count, per_seq * CAP, model_width), 'se...]
    pallas_call x0 -> x1, Pallas kernels: none -> 138 us  [run_experts(): pl.pallas_call(functools.partial(expert_kernel, n, zn), out_shape=(jax.Sh...]
    dot_general x21 -> x7, matrix products: 59.6 us -> 4.18 us  [the longest x5 3.7 us: dot(): return lax.dot_general(a, b, dims, preferred_element_type=F32)]
    convert_element_type x7 -> x2, other arithmetic: 19.3 us -> 0.01 us  [the longest x1 0.01 us: shards(): share_b = lax.optimization_barrier(shares.astype(BF16))]
    psum x1 -> x0, blocking collectives: 18.1 us -> none  [shards(): weight_grad = lax.psum(term_part, 'exp')]
    all_to_all x3 -> x0, starting transfers between devices: 17.3 us -> none  [the longest x1 7.56 us: shards(): lax.all_to_all(send_z.reshape(seq_count, per_seq * CAP, model_width), 'se...]
  transfers between devices with their start and end apart: 4 -> 0, of which waited for: 3 -> 0; matrix products, arithmetic and copies ran while one was open for 6% -> 0% of each run, Pallas kernels for 0% -> 0%
where the time goes in v1:
time: 304 us; the launch traced here: 303 us
  blocking collectives  142 us (47%)
  Pallas kernels  138 us (45%)
  other arithmetic  12.4 us (4%)
  local copies, waits for them, and re-layouts  6.4 us (2%)
  matrix products  4.18 us (1%)
    pallas_call x1, Pallas kernels, run_experts(): pl.pallas_call(functools.partial(expert_kernel, n, zn), out_shape=(jax.Sh...  138 us
    psum x1, blocking collectives, shards(): grad_router = lax.psum(router_part, 'seq')  126 us
    psum x1, blocking collectives, shards(): lax.psum((jnp.sum(norm_grad, axis=-1), jnp.sum(norm_grad * normed_cols, a...  15.3 us

profile of v1, /device:TPU:32, one launch (start us, length us, event | category | flops | bytes accessed | tf_op | source)
XLA Modules:
  0.0 303.1 jit_solution(5152929937212259662)
XLA Ops:
  0.7 1.5 convert_reduce_fusion
  2.2 1.7 fusion.2
  3.9 0.7 broadcast_add_fusion
  4.6 1.8 fusion
  6.4 0.4 fusion.6
  7.1 1.0 convolution_convert_fusion.1
  8.2 1.0 convolution_convert_fusion
  9.5 0.6 pad_maximum_fusion.2
  10.1 3.2 %pad_maximum_fusion.send = bf16[16,48,4224]{2,1,0:T(8,128)(2,1)} fusion(bf16[16,24,4224]{2,1,0:T(8,128)(2,1)S(1)} %bitcast.20, bf16[16,24,4224]{2,1,0:T(8,128)(2,1)S(1)} %bitcast.19), kind=kLoop, calls=%fused_computation | loop fusion | flops 12976128 | bytes 12976128 | tf_op jit(solution)/shard_map/concatenate | solution.py:483
  13.3 137.7 %shard_map.137 = (bf16[16,48,256]{2,1,0:T(8,128)(2,1)}, f32[8,128]{1,0:T(8,128)}, bf16[1,4096,128]{2,1,0:T(8,128)(2,1)}, bf16[1,4096,128]{2,1,0:T(8,128)(2,1)}, bf16[1,128,4096]{2,1,0:T(8,128)(2,1)}) custom-call(bf16[16,48,4224]{2,1,0:T(8,128)(2,1)} %pad_maximum_fusion.send, bf16[1,4096,128]{2,1,0:T(8,128)(2,1)} %gate.1, bf16[1,4096,128]{2,1,0:T(8,128)(2,1)} %up.1, ...), custom_call_target="tpu_custom_call" | custom-call | flops 6442450944 | bytes 16777216 | tf_op jit(solution)/shard_map/pallas_call | solution.py:408
  151.0 0.7 slice_bitcast_fusion
  151.7 0.2 select_reduce_fusion
  151.9 0.2 fusion.9
  152.1 126.3 %psum.23 = f32[512,16]{0,1:T(8,128)} all-reduce(f32[512,16]{0,1:T(8,128)S(1)} %fusion.9), channel_id=1, replica_groups=mesh['seq'=32,'exp'=8] {'seq'}, use_global_device_ids=true, to_apply=%region_15.16 | all-reduce | flops 8192 | bytes 65536 | tf_op jit(solution)/shard_map/psum | solution.py:506
  278.4 1.3 copy.24
  279.7 0.3 fusion.12
  280.1 0.9 dynamic-slice_add_fusion
  280.9 1.1 fusion.24
  282.0 15.3 %all-reduce = (f32[128]{0:T(128)S(1)}, f32[128]{0:T(128)}) all-reduce(f32[128]{0:T(128)S(1)} %get-tuple-element.16, f32[128]{0:T(128)S(1)} %get-tuple-element.15), channel_id=1, replica_groups=mesh['seq'=32,'exp'=8] {'exp'}, use_global_device_ids=true, to_apply=%region_14.15 | all-reduce | flops 256 | bytes 2048 | tf_op jit(solution)/shard_map/psum | solution.py:510
  297.4 0.7 broadcast_multiply_fusion
  298.1 0.8 subtract_multiply_fusion
  298.9 2.3 copy.29
  301.2 1.0 copy.30
  302.2 1.0 copy.31
  (29 shorter events, 0.8 us)
Async XLA Ops:
  0.6 5.7 %copy-start = (bf16[4096,16]{0,1:T(8,128)(2,1)S(1)}, bf16[4096,16]{0,1:T(8,128)(2,1)}, u32[]{:S(2)}) copy-start(bf16[4096,16]{0,1:T(8,128)(2,1)} %param.16) | copy-start | bytes 393220
  2.2 4.6 %copy-start.6 = (s32[128,2]{0,1:T(2,128)S(1)}, s32[128,2]{0,1:T(2,128)}, u32[]{:S(2)}) copy-start(s32[128,2]{0,1:T(2,128)} %param.12) | copy-start | bytes 3076
  6.4 1.8 copy-start.3
  6.4 1.8 copy-start.5
  7.1 2.1 copy-start.4
  280.1 22.1 %copy-start.1 = (bf16[1,128,4096]{2,1,0:T(8,128)(2,1)S(1)}, bf16[1,128,4096]{2,1,0:T(8,128)(2,1)}, u32[]{:S(2)}) copy-start(bf16[1,128,4096]{2,1,0:T(8,128)(2,1)} %get-tuple-element.40) | copy-start | bytes 3145732
  297.4 3.8 %copy-start.2 = (bf16[1,4096,128]{2,1,0:T(8,128)(2,1)S(1)}, bf16[1,4096,128]{2,1,0:T(8,128)(2,1)}, u32[]{:S(2)}) copy-start(bf16[1,4096,128]{2,1,0:T(8,128)(2,1)} %get-tuple-element.39) | copy-start | bytes 3145732

commit v2 on v1

--- a/solution.py
+++ b/solution.py
@@ -21,62 +21,33 @@
     return lax.dot_general(a, b, dims, preferred_element_type=F32)
 
 
-def expert_kernel(
-    n,
-    zn,
-    send,
-    gate,
-    up,
-    down,
-    back_out,
-    terms_out,
-    gate_out,
-    up_out,
-    down_out,
-    recv,
-    w_gate,
-    w_up,
-    w_down,
-    rows_z,
-    rows_wdy,
-    d_gu,
-    hid,
-    hr,
-    g_acc,
-    u_acc,
-    r_acc,
-    t_send,
-    t_recv,
-    b_send,
-    b_recv,
-    term_own,
-    term_z,
-    term_sum,
-    term_b,
-    gu_own,
-    gu_send,
-    gu_recv,
-    dn_own,
-    dn_send,
-    dn_recv,
-    w_local,
-    w_ssem,
-    w_rsem,
-    d_ssem,
-    d_rsem,
-    t_ssem,
-    t_rsem,
-    b_ssem,
-    b_rsem,
-    tz_ssem,
-    tz_rsem,
-    tb_ssem,
-    tb_rsem,
-    g_ssem,
-    g_rsem,
-    h_ssem,
-    h_rsem,
-):
+def split_refs(refs, counts):
+    parts, at = [], 0
+    for count in counts:
+        parts.append(refs[at : at + count])
+        at += count
+    return parts
+
+
+def split3(x):
+    hi = x.astype(BF16)
+    rest = x - hi.astype(F32)
+    mid = rest.astype(BF16)
+    return hi, mid, (rest - mid.astype(F32)).astype(BF16)
+
+
+def expert_kernel(n, zn, *refs):
+    (
+        (tokens, cotangent, ids, shift, scale, ada_gate, router, gate, up, down),
+        (input_out, router_out, gate_out, up_out, down_out),
+        (mod, og, place_t, send, recv, w_gate, w_up, w_down, rows_z, rows_wdy, d_gu, hid, hr),
+        (g_acc, u_acc, r_acc, t_send, t_recv, b_send, b_recv, term_own, term_z, term_sum, term_b),
+        (gu_own, gu_send, gu_recv, dn_own, dn_send, dn_recv),
+        (logit_acc, rc_own, rc_sib, rx_sum, rx_buf, ry_sum, ry_buf, ns_own, ns_z),
+        (w_local, w_ssem, w_rsem, d_ssem, d_rsem, t_ssem, t_rsem, b_ssem, b_rsem),
+        (tz_ssem, tz_rsem, tb_ssem, tb_rsem, g_ssem, g_rsem, h_ssem, h_rsem),
+        (rc_ssem, rc_rsem, rx_ssem, rx_rsem, ry_ssem, ry_rsem, ns_ssem, ns_rsem),
+    ) = split_refs(refs, (10, 5, 13, 11, 6, 9, 9, 8, 8))
     slots = n * n
     width = rows_z.shape[1]
     group = n * CAP
@@ -85,6 +56,7 @@
     nb = width // kb
     cols_z = width // zn
     half = cols_z // 2
+    toks = tokens.shape[0]
     seq = lax.axis_index("seq")
     z = lax.axis_index("exp")
     core = lax.rem(seq, 2)
@@ -130,6 +102,20 @@
 
     def tb_copy(slot):
         return remote(term_sum, term_b.at[slot], tb_ssem.at[slot], tb_rsem.at[slot], source(slot))
+
+    def rc_copy():
+        return remote(rc_own, rc_sib, rc_ssem.at[0], rc_rsem.at[0], sibling)
+
+    def rx_copy(step, at):
+        to = (2 * (cy * n + lax.rem(cx + step, n)) + core, z)
+        return remote(rx_sum, rx_buf.at[at], rx_ssem.at[step], rx_rsem.at[at], to)
+
+    def ry_copy(step, at):
+        to = (2 * (lax.rem(cy + step, n) * n + cx) + core, z)
+        return remote(ry_sum, ry_buf.at[at], ry_ssem.at[step], ry_rsem.at[at], to)
+
+    def ns_copy(step):
+        return remote(ns_own, ns_z.at[step], ns_ssem.at[step], ns_rsem.at[step], z_peer(step))
 
     def gu_copy(b):
         return remote(gu_send.at[b], gu_recv.at[b], g_ssem.at[b], g_rsem.at[b], sibling)
@@ -166,17 +152,97 @@
         lambda j: pl.semaphore_signal(barrier, inc=1, device_id=z_peer(j), device_id_type=MESH),
     )
     pl.semaphore_signal(barrier, inc=1, device_id=sibling, device_id_type=MESH)
-    own = pltpu.make_async_copy(send.at[0], recv.at[0], w_local.at[3])
-    own.start()
     for i in range(3):
         w_copy_local(i).start()
+
+    def moment(center):
+        def body(b, acc):
+            cols = pl.ds(pl.multiple_of(b * kb, kb), kb)
+            x = tokens[:, cols].astype(F32)
+            if center is not None:
+                x = (x - center) * (x - center)
+            return acc + jnp.sum(x, axis=1, keepdims=True)
+
+        return lax.fori_loop(0, nb, body, jnp.zeros((toks, 1), F32)) * (1.0 / width)
+
+    mean = moment(None)
+    inv_std = lax.rsqrt(moment(mean) + EPSILON)
+    logit_acc[...] = jnp.zeros_like(logit_acc)
+    experts = router.shape[1]
+
+    def modulate(b):
+        cols = pl.ds(pl.multiple_of(b * kb, kb), kb)
+        normed = (tokens[:, cols].astype(F32) - mean) * inv_std
+        m = (normed * (1.0 + scale[:, cols]) + shift[:, cols]).astype(BF16)
+        mod[:, cols] = m
+        og[:, cols] = (ada_gate[:, cols] * cotangent[:, cols].astype(F32)).astype(BF16)
+        logit_acc[:, :experts] += dot(m, router[cols, :])
+
+    loop(0, nb, modulate)
+    scores = jax.nn.sigmoid(logit_acc[...])
+    expert_at = lax.broadcasted_iota(jnp.int32, (toks, 128), 1)
+    hits = [expert_at == ids[:, k : k + 1] for k in range(2)]
+    picked = [jnp.sum(jnp.where(h, scores, 0.0), axis=1, keepdims=True) for h in hits]
+    score_sum = picked[0] + picked[1]
+    shares = [p / score_sum for p in picked]
+    share_r = [s.astype(BF16).astype(F32) for s in shares]
+    routed = jnp.where(hits[0] | hits[1], 1.0, 0.0)
+    tok_at = lax.broadcasted_iota(jnp.int32, (toks, toks), 0)
+    earlier = jnp.where(tok_at > lax.broadcasted_iota(jnp.int32, (toks, toks), 1), 1.0, 0.0)
+    rank = dot(earlier.astype(BF16), routed.astype(BF16))
+    bits = n.bit_length() - 1
+    e_dy = ((expert_at >> bits) - cy) & (n - 1)
+    e_dx = ((expert_at & (n - 1)) - cx) & (n - 1)
+    base = ((((e_dx - e_dy) & (n - 1)) * n + e_dy) * CAP).astype(F32) + rank
+    slot_at = lax.broadcasted_iota(jnp.int32, (toks, slots * CAP), 1).astype(F32)
+    places = [
+        jnp.where(slot_at == jnp.sum(jnp.where(h, base, 0.0), axis=1, keepdims=True), 1.0, 0.0)
+        for h in hits
+    ]
+    place_t[...] = (places[0] + places[1]).T.astype(BF16)
+    slot_share = jnp.sum(
+        (places[0] * share_r[0] + places[1] * share_r[1]).T, axis=1, keepdims=True
+    )
+    side = jnp.broadcast_to(slot_share, (slots * CAP, 128))
+    for k in range(slots):
+        part = side[k * CAP : (k + 1) * CAP]
+        pair = jnp.concatenate([part, part], axis=0).astype(BF16)
+        send[k, :, width : width + 128] = pair
+        if k == 0:
+            recv[0, :, width : width + 128] = pair
+
+    hr[...] = jnp.zeros_like(hr)
     pl.semaphore_wait(barrier, slots + zn - 1)
-
     for i in range(3):
         w_copy(i).start()
-    loop(1, slots, lambda k: send_copy(k).start())
-    hr[...] = jnp.zeros_like(hr)
-    own.wait()
+
+    def dispatch_group(g):
+        rows = pl.ds(pl.multiple_of(g * group, group), group)
+
+        def fill(b):
+            cols = pl.ds(pl.multiple_of(b * kb, kb), kb)
+            zc = dot(place_t[rows, :], mod[:, cols])
+            dc = dot(place_t[rows, :], og[:, cols])
+            for i in range(n):
+                at = slice(i * CAP, (i + 1) * CAP)
+                pair = jnp.concatenate([zc[at], dc[at]], axis=0).astype(BF16)
+                send[g * n + i, :, cols] = pair
+                if i == 0:
+
+                    @pl.when(g == 0)
+                    def _():
+                        recv[0, :, cols] = pair
+
+        loop(0, nb, fill)
+
+        def start(i):
+            @pl.when(g * n + i > 0)
+            def _():
+                send_copy(g * n + i).start()
+
+        loop(0, n, start)
+
+    loop(0, n, dispatch_group)
     for i in range(3):
         w_copy_local(i).wait()
         w_copy(i).wait()
@@ -304,6 +370,26 @@
     term_sum[...] = total
     loop(1, slots, lambda k: tb_copy(k).start())
     loop(nb // 2, nb, weight_grads)
+    loop(1, slots, lambda k: tb_copy(k).wait_recv())
+    flat = lax.broadcasted_iota(jnp.int32, (8, 128), 0) * 128 + lax.broadcasted_iota(
+        jnp.int32, (8, 128), 1
+    )
+    terms = jnp.where(flat < CAP, term_sum[...], 0.0)
+    for k in range(1, slots):
+        terms = jnp.where((flat >= k * CAP) & (flat < (k + 1) * CAP), term_b[k], terms)
+    term_row = jnp.concatenate([terms[i : i + 1] for i in range(nt)], axis=1)[:, : slots * CAP]
+    choice = [jnp.sum(p * term_row, axis=1, keepdims=True) for p in places]
+    mean_grad = shares[0] * choice[0] + shares[1] * choice[1]
+    logit_grad = jnp.zeros((toks, 128), F32)
+    for k in range(2):
+        pick = (choice[k] - mean_grad) / score_sum * picked[k] * (1.0 - picked[k])
+        logit_grad = logit_grad + jnp.where(hits[k], pick, 0.0)
+    my_cols = pl.ds(pl.multiple_of(z * cols_z, cols_z), cols_z)
+    lg_rows = logit_grad.T[:16]
+    parts = [p.astype(F32) for p in split3(lg_rows)]
+    prod = dot(jnp.concatenate(parts, axis=0).astype(BF16), mod[:, my_cols])
+    rc_own[...] = prod[:16] + prod[16:32] + prod[32:]
+    rc_copy().start()
     reduce_group(n - 1)
 
     def finish(b):
@@ -315,19 +401,58 @@
         up_out[0, cols, :] = gu[:, hidden:].astype(BF16)
         down_out[0, :, cols] = (dn_own[b] + dn_recv[b].astype(F32)).astype(BF16)
 
-    loop(0, nb, finish)
-
-    loop(1, slots, lambda k: tb_copy(k).wait_recv())
-    flat = lax.broadcasted_iota(jnp.int32, (8, 128), 0) * 128 + lax.broadcasted_iota(
-        jnp.int32, (8, 128), 1
-    )
-    terms = jnp.where(flat < CAP, term_sum[...], 0.0)
-    for k in range(1, slots):
-        terms = jnp.where((flat >= k * CAP) & (flat < (k + 1) * CAP), term_b[k], terms)
-    terms_out[...] = terms
+    rc_copy().wait_recv()
+    rx_sum[...] = rc_own[...] + rc_sib[...]
+    rx_buf[cx] = rx_sum[...]
+    loop(1, n, lambda j: rx_copy(j, cx).start())
+    loop(0, nb // 2, finish)
+    loop(1, n, lambda j: rx_copy(j, lax.rem(cx + j, n)).wait_recv())
+    total = rx_buf[0]
+    for j in range(1, n):
+        total = total + rx_buf[j]
+    ry_sum[...] = total
+    ry_buf[cy] = total
+    loop(1, n, lambda j: ry_copy(j, cy).start())
+    loop(nb // 2, nb, finish)
+
+    def mod_part(i):
+        return dot(split3(logit_grad)[i][:, :experts], router[my_cols, :], NT)
+
+    mod_grad = mod_part(0) + mod_part(1) + mod_part(2)
+    gain = 1.0 + scale[:, my_cols]
+    normed = (tokens[:, my_cols].astype(F32) - mean) * inv_std
 
     loop(1, slots, lambda k: b_copy(k).wait_recv())
-    back_out[...] = b_recv[...]
+    tiles = [b_recv[k].astype(F32) for k in range(slots)]
+    rows_back = jnp.concatenate(
+        [
+            jnp.concatenate([t[:CAP] for t in tiles], axis=0),
+            jnp.concatenate([t[CAP:] for t in tiles], axis=0),
+        ],
+        axis=1,
+    ).astype(BF16)
+    norm_grad = (mod_grad + dot(place_t[...], rows_back, TN)) * gain
+    sums = [
+        jnp.sum(norm_grad, axis=1, keepdims=True),
+        jnp.sum(norm_grad * normed, axis=1, keepdims=True),
+    ]
+    lane = lax.broadcasted_iota(jnp.int32, (toks, 128), 1)
+    sums_t = jnp.where(lane == 0, sums[0], jnp.where(lane == 1, sums[1], 0.0)).T
+    ns_own[...] = sums_t[:8]
+    loop(1, zn, lambda j: ns_copy(j).start())
+
+    loop(1, n, lambda j: ry_copy(j, lax.rem(cy + j, n)).wait_recv())
+    total = ry_buf[0]
+    for j in range(1, n):
+        total = total + ry_buf[j]
+    router_out[...] = total
+
+    loop(1, zn, lambda j: ns_copy(j).wait_recv())
+    total = ns_own[...]
+    for j in range(1, zn):
+        total = total + ns_z[j]
+    total = jnp.concatenate([total, jnp.zeros((120, toks), F32)], axis=0).T * (1.0 / width)
+    input_out[...] = inv_std * (norm_grad - total[:, 0:1] - normed * total[:, 1:2])
 
     def drain_slot(k):
         send_copy(k).wait_send()
@@ -336,8 +461,16 @@
 
     loop(1, slots, drain_slot)
 
+    def drain_ring(j):
+        rx_copy(j, cx).wait_send()
+        ry_copy(j, cy).wait_send()
+
+    rc_copy().wait_send()
+    loop(1, n, drain_ring)
+
     def drain_z(j):
         tz_copy(j).wait_send()
+        ns_copy(j).wait_send()
         loop(0, n, lambda g: t_copy(g, j).wait_send())
 
     loop(1, zn, drain_z)
@@ -349,9 +482,24 @@
     loop(0, nb, drain_b)
 
 
-def run_experts(n, zn, send, gate, up, down):
+def shards(
+    tokens,
+    cotangent,
+    expert_ids,
+    ada_shift,
+    ada_scale,
+    ada_gate,
+    router_weight,
+    gate_blocks,
+    up_blocks,
+    down_blocks,
+):
+    zn = lax.axis_size("exp")
+    n = math.isqrt(lax.axis_size("seq") // 2)
     slots = n * n
-    width, hidden = gate.shape[1], gate.shape[2]
+    toks, width = tokens.shape
+    experts = router_weight.shape[1]
+    hidden = gate_blocks.shape[2]
     rows = slots * CAP
     cols_z = width // zn
     nb = width // 512
@@ -359,7 +507,11 @@
     dma = pltpu.SemaphoreType.DMA
     vm = pltpu.VMEM
     scratch = [
-        vm(send.shape, BF16),
+        vm((toks, width), BF16),
+        vm((toks, width), BF16),
+        vm((rows, toks), BF16),
+        vm((slots, 2 * CAP, width + 128), BF16),
+        vm((slots, 2 * CAP, width + 128), BF16),
         vm((2, width, hidden), BF16),
         vm((2, width, hidden), BF16),
         vm((2, hidden, width), BF16),
@@ -385,135 +537,54 @@
         vm((nb, hidden, 512), F32),
         vm((nb, hidden, 512), BF16),
         vm((nb, hidden, 512), BF16),
-        dma((4,)),
-        dma((3,)),
-        dma((3,)),
-        dma((slots,)),
-        dma((slots,)),
-        dma((n, zn)),
-        dma((n, zn)),
-        dma((slots,)),
-        dma((slots,)),
-        dma((zn,)),
-        dma((zn,)),
-        dma((slots,)),
-        dma((slots,)),
-        dma((nb,)),
-        dma((nb,)),
-        dma((nb,)),
-        dma((nb,)),
+        vm((toks, 128), F32),
+        vm((16, cols_z), F32),
+        vm((16, cols_z), F32),
+        vm((16, cols_z), F32),
+        vm((n, 16, cols_z), F32),
+        vm((16, cols_z), F32),
+        vm((n, 16, cols_z), F32),
+        vm((8, toks), F32),
+        vm((zn, 8, toks), F32),
     ]
+    sems = [3, 3, 3, slots, slots, (n, zn), (n, zn), slots, slots]
+    sems += [zn, zn, slots, slots, nb, nb, nb, nb]
+    sems += [1, 1, n, n, n, n, zn, zn]
+    scratch += [dma(s if isinstance(s, tuple) else (s,)) for s in sems]
     any_spec = pl.BlockSpec(memory_space=pl.ANY)
     vm_spec = pl.BlockSpec(memory_space=pltpu.VMEM)
-    return pl.pallas_call(
+    row = lambda v: v.reshape(1, width)
+    grad_input, router_t, grad_gate, grad_up, grad_down = pl.pallas_call(
         functools.partial(expert_kernel, n, zn),
         out_shape=(
-            jax.ShapeDtypeStruct((slots, 2 * CAP, cols_z // 2), BF16),
-            jax.ShapeDtypeStruct((8, 128), F32),
+            jax.ShapeDtypeStruct((toks, cols_z), F32),
+            jax.ShapeDtypeStruct((16, cols_z), F32),
             jax.ShapeDtypeStruct((1, width, hidden), BF16),
             jax.ShapeDtypeStruct((1, width, hidden), BF16),
             jax.ShapeDtypeStruct((1, hidden, width), BF16),
         ),
-        in_specs=[any_spec] * 4,
+        in_specs=[vm_spec] * 7 + [any_spec] * 3,
         out_specs=(vm_spec,) * 5,
         scratch_shapes=scratch,
         compiler_params=pltpu.CompilerParams(
-            collective_id=0, has_side_effects=True, vmem_limit_bytes=58 * 1024 * 1024
+            collective_id=0, has_side_effects=True, vmem_limit_bytes=60 * 1024 * 1024
         ),
         cost_estimate=pl.CostEstimate(
             flops=16 * rows * width * 2 * hidden, bytes_accessed=16 * 1024 * 1024, transcendentals=0
         ),
-    )(send, gate, up, down)
-
-
-def shards(
-    tokens,
-    cotangent,
-    expert_ids,
-    ada_shift,
-    ada_scale,
-    ada_gate,
-    router_weight,
-    gate_blocks,
-    up_blocks,
-    down_blocks,
-):
-    zn = lax.axis_size("exp")
-    experts = lax.axis_size("seq") // 2
-    n = math.isqrt(experts)
-    seq_index = lax.axis_index("seq")
-    exp_index = lax.axis_index("exp")
-    tok_rows, width = tokens.shape
-    cols = width // zn
-    slots = n * n
-    highest = lax.Precision.HIGHEST
-    col_start = exp_index * cols
-
-    values = tokens.astype(F32)
-    center = values - jnp.mean(values, axis=-1, keepdims=True)
-    inv_std = lax.rsqrt(jnp.mean(center * center, axis=-1, keepdims=True) + EPSILON)
-    normed = center * inv_std
-    modulated = (normed * (1.0 + ada_scale) + ada_shift).astype(BF16)
-    scores = jax.nn.sigmoid(dot(modulated, router_weight))
-    expert_iota = jnp.arange(experts, dtype=jnp.int32)
-    chosen = (expert_ids[:, :, None] == expert_iota[None, None, :]).astype(F32)
-    picked = jnp.sum(chosen * scores[:, None, :], axis=-1)
-    score_sum = jnp.sum(picked, axis=-1, keepdims=True)
-    shares = picked / score_sum
-    share_b = lax.optimization_barrier(shares.astype(BF16))
-    out_grad = (ada_gate * cotangent.astype(F32)).astype(BF16)
-
-    routed = jnp.sum(chosen, axis=1)
-    tok_iota = jnp.arange(tok_rows, dtype=jnp.int32)
-    earlier = (tok_iota[:, None] > tok_iota[None, :]).astype(BF16)
-    rank_all = dot(earlier, routed.astype(BF16))
-    rank = jnp.sum(chosen * rank_all[:, None, :], axis=-1).astype(jnp.int32)
-    chip = seq_index // 2
-    dy = lax.rem(expert_ids // n - chip // n + n, n)
-    dx = lax.rem(lax.rem(expert_ids, n) - lax.rem(chip, n) + n, n)
-    slot = (lax.rem(dx - dy + n, n) * n + dy) * CAP + rank
-    slot_iota = jnp.arange(slots * CAP, dtype=jnp.int32)
-    hit = slot[:, :, None] == slot_iota[None, None, :]
-    place = jnp.any(hit, axis=1).astype(BF16)
-    slot_share = jnp.sum(jnp.where(hit, share_b.astype(F32)[:, :, None], 0.0), axis=(0, 1))
-
-    send_z = dot(place, modulated, TN).astype(BF16)
-    send_dy = dot(place, out_grad, TN).astype(BF16)
-    side = jnp.broadcast_to(slot_share.astype(BF16)[:, None], (slots * CAP, 128))
-    send = jnp.concatenate(
-        [
-            jnp.concatenate([send_z, side], axis=1).reshape(slots, CAP, width + 128),
-            jnp.concatenate([send_dy, side], axis=1).reshape(slots, CAP, width + 128),
-        ],
-        axis=1,
+    )(
+        tokens,
+        cotangent,
+        expert_ids,
+        row(ada_shift),
+        row(ada_scale),
+        row(ada_gate),
+        router_weight,
+        gate_blocks,
+        up_blocks,
+        down_blocks,
     )
-    back, terms, grad_gate, grad_up, grad_down = run_experts(
-        n, zn, send, gate_blocks, up_blocks, down_blocks
-    )
-    rows_back = (
-        back.reshape(slots, 2, CAP, cols // 2).transpose(0, 2, 1, 3).reshape(slots * CAP, cols)
-    )
-    expert_grad = dot(place, rows_back)
-    term_row = terms.reshape(-1)[: slots * CAP]
-    choice_grad = jnp.sum(jnp.where(hit, term_row[None, None, :], 0.0), axis=-1)
-    mean_grad = jnp.sum(shares * choice_grad, axis=-1, keepdims=True)
-    pick_grad = (choice_grad - mean_grad) / score_sum * picked * (1.0 - picked)
-    logit_grad = jnp.sum(chosen * pick_grad[:, :, None], axis=1)
-    router_cols = lax.dynamic_slice_in_dim(router_weight, col_start, cols, 0).astype(F32)
-    modulated_cols = lax.dynamic_slice_in_dim(modulated, col_start, cols, 1).astype(F32)
-    mod_grad = expert_grad + lax.dot_general(logit_grad, router_cols, NT, precision=highest)
-    router_part = lax.dot_general(modulated_cols, logit_grad, TN, precision=highest)
-    grad_router = lax.psum(router_part, "seq")
-    scale_cols = lax.dynamic_slice_in_dim(ada_scale, col_start, cols, 0)
-    normed_cols = lax.dynamic_slice_in_dim(normed, col_start, cols, 1)
-    norm_grad = mod_grad * (1.0 + scale_cols)
-    grad_total, grad_cross = lax.psum(
-        (jnp.sum(norm_grad, axis=-1), jnp.sum(norm_grad * normed_cols, axis=-1)), "exp"
-    )
-    grad_input = inv_std * (
-        norm_grad - grad_total[:, None] / width - normed_cols * (grad_cross[:, None] / width)
-    )
-    return (grad_input, grad_router, grad_gate, grad_up, grad_down)
+    return (grad_input, router_t[:experts].T, grad_gate, grad_up, grad_down)
 
 
 def solution(mesh):

time: 304 us -> 166 us (0.55)
  blocking collectives: 142 us -> 0 us
  Pallas kernels: 138 us -> 153 us
  other arithmetic: 12.4 us -> 0 us
  local copies, waits for them, and re-layouts: 6.4 us -> 10.9 us
  matrix products: 4.18 us -> 0 us
    psum x2 -> x0, blocking collectives: 142 us -> none  [the longest x1 126 us: shards(): grad_router = lax.psum(router_part, 'seq')]
    pallas_call x1, Pallas kernels: 138 us -> 153 us  [shards(): pl.pallas_call(functools.partial(expert_kernel, n, zn), out_shape=(jax.Sh...]
    unnamed x18 -> x15, local copies, waits for them, and re-layouts: 4.31 us -> 10.9 us
    dot_general x7 -> x0, matrix products: 4.18 us -> none  [the longest x5 3.7 us: dot(): return lax.dot_general(a, b, dims, preferred_element_type=F32)]
    concatenate x2 -> x0, other arithmetic: 3.74 us -> none  [the longest x1 3.15 us: shards(): jnp.concatenate([jnp.concatenate([send_z, side], axis=1).reshape(slots, C...]
    reduce_sum x8 -> x0, other arithmetic: 3.55 us -> none  [the longest x1 1.66 us: shards(): jnp.mean(center * center, axis=-1, keepdims=True) + EPSILON]
where the time goes in v2:
time: 166 us; the launch traced here: 165 us
  Pallas kernels  153 us (92%)
  local copies, waits for them, and re-layouts  10.9 us (7%)
    pallas_call x1, Pallas kernels, shards(): pl.pallas_call(functools.partial(expert_kernel, n, zn), out_shape=(jax.Sh...  153 us
    unnamed x15, local copies, waits for them, and re-layouts  10.9 us

profile of v2, /device:TPU:32, one launch (start us, length us, event | category | flops | bytes accessed | tf_op | source)
XLA Modules:
  0.0 164.7 jit_solution(2416837475158557861)
XLA Ops:
  0.6 0.0 copy-start.3
  0.6 0.7 copy-done.3
  1.3 0.7 copy.15.refs_2_
  2.1 2.2 %copy.16.refs_6_ = bf16[4096,16]{1,0:T(8,128)(2,1)} copy(bf16[4096,16]{0,1:T(8,128)(2,1)} %param.16) | data formatting | bytes 262144 | tf_op args[6]
  4.3 153.2 %shard_map.137 = (f32[128,512]{1,0:T(8,128)}, f32[16,512]{1,0:T(8,128)}, bf16[1,4096,128]{2,1,0:T(8,128)(2,1)}, bf16[1,4096,128]{2,1,0:T(8,128)(2,1)}, bf16[1,128,4096]{2,1,0:T(8,128)(2,1)}) custom-call(bf16[128,4096]{1,0:T(8,128)(2,1)} %refs_0_.1, bf16[128,4096]{1,0:T(8,128)(2,1)} %refs_1_.1, s32[128,2]{1,0:T(8,128)} %copy.15.refs_2_, f32[1,4096]{1,0:T(1,128)} %bitcast.5, ...), custom_call_target="tpu_custom_call" | custom-call | flops 6442450944 | bytes 16777216 | tf_op jit(solution)/shard_map/pallas_call | solution.py:557
  157.5 0.0 copy-start.2
  157.5 1.7 %copy.22 = f32[128,512]{1,0:T(8,128)} copy(f32[128,512]{1,0:T(8,128)} %get-tuple-element.20) | data formatting | bytes 524288
  159.2 0.0 copy-done.2
  159.2 0.6 copy.23
  159.8 0.0 copy-start.1
  159.8 2.4 %copy.24 = bf16[1,4096,128]{2,1,0:T(8,128)(2,1)} copy(bf16[1,4096,128]{2,1,0:T(8,128)(2,1)} %get-tuple-element.22) | data formatting | bytes 2097152
  162.1 0.0 copy-done.1
  162.1 0.0 copy-start
  162.1 1.0 copy.25
  163.1 0.6 copy-done
  163.7 1.0 copy.26
Async XLA Ops:
  0.6 0.7 copy-start.3
  157.5 1.7 %copy-start.2 = (f32[16,512]{1,0:T(8,128)S(1)}, f32[16,512]{1,0:T(8,128)}, u32[]{:S(2)}) copy-start(f32[16,512]{1,0:T(8,128)} %get-tuple-element.11) | copy-start | bytes 98308
  159.8 2.4 %copy-start.1 = (bf16[1,4096,128]{2,1,0:T(8,128)(2,1)S(1)}, bf16[1,4096,128]{2,1,0:T(8,128)(2,1)}, u32[]{:S(2)}) copy-start(bf16[1,4096,128]{2,1,0:T(8,128)(2,1)} %get-tuple-element.23) | copy-start | bytes 3145732
  162.1 1.6 copy-start

commit v3 on v2

--- a/solution.py
+++ b/solution.py
@@ -9,6 +9,10 @@
 from jax.sharding import PartitionSpec as P
 
 CAP = 24
+RELAYED = 2
+ROLE = (1, 7, 4, 2, 5)
+CLASS = (0, 0, 1, 1, 2)
+SIGN = (1, -1, 1, -1, -1)
 EPSILON = 1e-06
 MESH = pl.DeviceIdType.MESH
 F32 = jnp.float32
@@ -41,20 +45,21 @@
         (tokens, cotangent, ids, shift, scale, ada_gate, router, gate, up, down),
         (input_out, router_out, gate_out, up_out, down_out),
         (mod, og, place_t, send, recv, w_gate, w_up, w_down, rows_z, rows_wdy, d_gu, hid, hr),
-        (g_acc, u_acc, r_acc, t_send, t_recv, b_send, b_recv, term_own, term_z, term_sum, term_b),
+        (gu_acc, r_acc, t_send, t_in, t_own, m_send, m_in, b_send, b_recv),
+        (term_own, term_z, term_sum, term_b, sh_own, sh_recv, sh_col),
         (gu_own, gu_send, gu_recv, dn_own, dn_send, dn_recv),
         (logit_acc, rc_own, rc_sib, rx_sum, rx_buf, ry_sum, ry_buf, ns_own, ns_z),
-        (w_local, w_ssem, w_rsem, d_ssem, d_rsem, t_ssem, t_rsem, b_ssem, b_rsem),
+        (w_local, w_ssem, w_rsem, d_ssem, d_rsem, f_ssem, f_rsem, a_ssem, a_rsem),
+        (m_ssem, m_rsem, b_ssem, b_rsem, sh_ssem, sh_rsem),
         (tz_ssem, tz_rsem, tb_ssem, tb_rsem, g_ssem, g_rsem, h_ssem, h_rsem),
         (rc_ssem, rc_rsem, rx_ssem, rx_rsem, ry_ssem, ry_rsem, ns_ssem, ns_rsem),
-    ) = split_refs(refs, (10, 5, 13, 11, 6, 9, 9, 8, 8))
+    ) = split_refs(refs, (10, 5, 13, 9, 7, 6, 9, 9, 6, 8, 8))
     slots = n * n
     width = rows_z.shape[1]
     group = n * CAP
     hidden = w_gate.shape[2]
-    kb = 512
-    nb = width // kb
-    cols_z = width // zn
+    kb = cols_z = width // zn
+    nb = zn
     half = cols_z // 2
     toks = tokens.shape[0]
     seq = lax.axis_index("seq")
@@ -86,13 +91,39 @@
             src_ref=src, dst_ref=dst, send_sem=ssem, recv_sem=rsem, device_id=dev, device_id_type=MESH
         )
 
-    def send_copy(slot):
-        return remote(send.at[slot], recv.at[slot], d_ssem.at[slot], d_rsem.at[slot], target(slot))
-
-    def t_copy(g, step):
-        return remote(
-            t_send.at[g, step], t_recv.at[g, step], t_ssem.at[g, step], t_rsem.at[g, step], z_peer(step)
-        )
+    def plane(step):
+        return lax.rem(z + step + 2 * zn, zn)
+
+    def turn(g):
+        return 1 - 2 * lax.rem(g, 2)
+
+    def own_class(g, c):
+        return plane(-3 * turn(g) * c)
+
+    def direct_copy(slot):
+        dst = recv.at[slot // n, :, lax.rem(slot, n)]
+        return remote(send.at[slot], dst, d_ssem.at[slot, 0], d_rsem.at[slot, 0], target(slot))
+
+    def part_copy(slot, c):
+        g = slot // n
+        r = own_class(g, c)
+        dst = recv.at[g, r, lax.rem(slot, n)]
+        return remote(send.at[slot, r], dst, d_ssem.at[slot, c], d_rsem.at[slot, c], target(slot))
+
+    def relay_copy(g, i, r):
+        to = (seq, plane(turn(g) * SIGN[i]))
+        return remote(recv.at[g, r], recv.at[g, r], f_ssem.at[g, i], f_rsem.at[g, i], to)
+
+    def near_copy(g, i):
+        to = (seq, plane(-turn(g) * SIGN[i]))
+        return remote(t_send.at[g, i], t_in.at[g, i], a_ssem.at[g, i], a_rsem.at[g, i], to)
+
+    def far_copy(g, c):
+        to = (seq, own_class(g, c))
+        return remote(m_send.at[g, c - 1], m_in.at[g, c - 1], m_ssem.at[g, c - 1], m_rsem.at[g, c - 1], to)
+
+    def sh_copy(slot):
+        return remote(sh_own, sh_recv.at[slot], sh_ssem.at[slot], sh_rsem.at[slot], target(slot))
 
     def b_copy(slot):
         return remote(b_send.at[slot], b_recv.at[slot], b_ssem.at[slot], b_rsem.at[slot], source(slot))
@@ -168,7 +199,7 @@
     mean = moment(None)
     inv_std = lax.rsqrt(moment(mean) + EPSILON)
     logit_acc[...] = jnp.zeros_like(logit_acc)
-    experts = router.shape[1]
+    experts = router.shape[0]
 
     def modulate(b):
         cols = pl.ds(pl.multiple_of(b * kb, kb), kb)
@@ -176,12 +207,13 @@
         m = (normed * (1.0 + scale[:, cols]) + shift[:, cols]).astype(BF16)
         mod[:, cols] = m
         og[:, cols] = (ada_gate[:, cols] * cotangent[:, cols].astype(F32)).astype(BF16)
-        logit_acc[:, :experts] += dot(m, router[cols, :])
+        logit_acc[:, :experts] += dot(m, router[:, cols], NT)
 
     loop(0, nb, modulate)
     scores = jax.nn.sigmoid(logit_acc[...])
     expert_at = lax.broadcasted_iota(jnp.int32, (toks, 128), 1)
-    hits = [expert_at == ids[:, k : k + 1] for k in range(2)]
+    ids_t = jnp.concatenate([ids[...].astype(F32), jnp.zeros((126, toks), F32)], axis=0).T
+    hits = [expert_at.astype(F32) == ids_t[:, k : k + 1] for k in range(2)]
     picked = [jnp.sum(jnp.where(h, scores, 0.0), axis=1, keepdims=True) for h in hits]
     score_sum = picked[0] + picked[1]
     shares = [p / score_sum for p in picked]
@@ -200,72 +232,123 @@
         for h in hits
     ]
     place_t[...] = (places[0] + places[1]).T.astype(BF16)
-    slot_share = jnp.sum(
-        (places[0] * share_r[0] + places[1] * share_r[1]).T, axis=1, keepdims=True
+    nt = hr.shape[0] // 128
+    flat = lax.broadcasted_iota(jnp.int32, (8, 128), 0) * 128 + lax.broadcasted_iota(
+        jnp.int32, (8, 128), 1
     )
-    side = jnp.broadcast_to(slot_share, (slots * CAP, 128))
-    for k in range(slots):
-        part = side[k * CAP : (k + 1) * CAP]
-        pair = jnp.concatenate([part, part], axis=0).astype(BF16)
-        send[k, :, width : width + 128] = pair
-        if k == 0:
-            recv[0, :, width : width + 128] = pair
+
+    def merge(own, others):
+        out = jnp.where(flat < CAP, own, 0.0)
+        for k in range(1, slots):
+            out = jnp.where((flat >= k * CAP) & (flat < (k + 1) * CAP), others[k], out)
+        return out
+
+    share_row = jnp.sum(places[0] * share_r[0] + places[1] * share_r[1], axis=0, keepdims=True)
+    if nt * 128 > slots * CAP:
+        share_row = jnp.concatenate(
+            [share_row, jnp.zeros((1, nt * 128 - slots * CAP), F32)], axis=1
+        )
+    sh_own[...] = jnp.zeros_like(sh_own)
+    for i in range(nt):
+        sh_own[i : i + 1, :] = share_row[:, 128 * i : 128 * (i + 1)]
 
     hr[...] = jnp.zeros_like(hr)
     pl.semaphore_wait(barrier, slots + zn - 1)
     for i in range(3):
         w_copy(i).start()
 
-    def dispatch_group(g):
+    loop(1, slots, lambda k: sh_copy(k).start())
+
+    def fill(g, b):
         rows = pl.ds(pl.multiple_of(g * group, group), group)
-
-        def fill(b):
-            cols = pl.ds(pl.multiple_of(b * kb, kb), kb)
-            zc = dot(place_t[rows, :], mod[:, cols])
-            dc = dot(place_t[rows, :], og[:, cols])
-            for i in range(n):
-                at = slice(i * CAP, (i + 1) * CAP)
-                pair = jnp.concatenate([zc[at], dc[at]], axis=0).astype(BF16)
-                send[g * n + i, :, cols] = pair
-                if i == 0:
-
-                    @pl.when(g == 0)
-                    def _():
-                        recv[0, :, cols] = pair
-
-        loop(0, nb, fill)
-
-        def start(i):
+        cols = pl.ds(pl.multiple_of(b * kb, kb), kb)
+        zc = dot(place_t[rows, :], mod[:, cols])
+        dc = dot(place_t[rows, :], og[:, cols])
+        for i in range(n):
+            at = slice(i * CAP, (i + 1) * CAP)
+            pair = jnp.concatenate([zc[at], dc[at]], axis=0).astype(BF16)
+
             @pl.when(g * n + i > 0)
             def _():
-                send_copy(g * n + i).start()
-
-        loop(0, n, start)
-
-    loop(0, n, dispatch_group)
+                send[g * n + i, b] = pair
+
+            if i == 0:
+
+                @pl.when(g == 0)
+                def _():
+                    recv[0, b, 0] = pair
+
+    def each_remote(g, body):
+        def one(i):
+            @pl.when(g * n + i > 0)
+            def _():
+                body(g * n + i)
+
+        loop(0, n, one)
+
+    def relayed_start(g):
+        for c in range(3):
+            fill(g, own_class(g, c))
+            each_remote(g, lambda slot: part_copy(slot, c).start())
+
+    def relayed_arrive(g):
+        for c in range(3):
+            each_remote(g, lambda slot: part_copy(slot, c).wait_recv())
+            for i in range(5):
+                if CLASS[i] == c:
+                    relay_copy(g, i, own_class(g, c)).start()
+
+    loop(0, RELAYED, relayed_start)
+    loop(RELAYED, n, lambda g: loop(0, nb, lambda b: fill(g, b)))
+    for g in range(RELAYED):
+        relayed_arrive(g)
+        if g == 0:
+            loop(RELAYED * n, (RELAYED + 1) * n, lambda k: direct_copy(k).start())
+    loop(1, slots, lambda k: sh_copy(k).wait_recv())
+    shares_in = merge(sh_own[...], sh_recv)
+    shares_in = jnp.concatenate([shares_in, jnp.zeros((120, 128), F32)], axis=0).T
+    for i in range(nt):
+        sh_col[128 * i : 128 * (i + 1), :] = jnp.broadcast_to(shares_in[:, i : i + 1], (128, 128))
     for i in range(3):
         w_copy_local(i).wait()
         w_copy(i).wait()
 
     def wait_group(g):
-        def one(i):
-            slot = g * n + i
-
-            @pl.when(slot > 0)
-            def _():
-                send_copy(slot).wait_recv()
-
-        loop(0, n, one)
-
-    def reduce_group(g):
-        loop(1, zn, lambda j: t_copy(g, j).wait_recv())
+        @pl.when(g < RELAYED)
+        def _():
+            for i in range(5):
+                relay_copy(g, i, plane(-turn(g) * ROLE[i])).wait_recv()
+
+        @pl.when(g >= RELAYED)
+        def _():
+            loop(0, n, lambda i: direct_copy(g * n + i).wait_recv())
+
+        @pl.when(g == RELAYED - 1)
+        def _():
+            loop((RELAYED + 1) * n, slots, lambda k: direct_copy(k).start())
+
+    def near_sums(g):
+        for i in range(5):
+            near_copy(g, i).wait_recv()
+        for c in (1, 2, 0):
+            total = t_own[g, c]
+            for i in range(5):
+                if CLASS[i] == c:
+                    total = total + t_in[g, i].astype(F32)
+            if c > 0:
+                m_send[g, c - 1] = total.astype(BF16)
+                far_copy(g, c).start()
+            else:
+                t_own[g, 0] = total
+
+    def far_sums(g):
+        for c in (1, 2):
+            far_copy(g, c).wait_recv()
+        total = t_own[g, 0] + m_in[g, 0].astype(F32) + m_in[g, 1].astype(F32)
         for i in range(n):
             slot = g * n + i
-            parts = []
-            for lo in (0, half):
-                part = t_recv[g, :, :, lo : lo + half].astype(F32)[:, i * CAP : (i + 1) * CAP, :]
-                parts.append(jnp.sum(part, axis=0))
-            packed = jnp.concatenate(parts, axis=0).astype(BF16)
+            part = total[i * CAP : (i + 1) * CAP]
+            packed = jnp.concatenate([part[:, :half], part[:, half:]], axis=0).astype(BF16)
             if i > 0:
                 b_send[slot] = packed
                 b_copy(slot).start()
@@ -283,27 +366,24 @@
     def compute_group(g):
         wait_group(g)
         rows = pl.ds(pl.multiple_of(g * group, group), group)
-        share = jnp.concatenate(
-            [recv[g * n + i, :, width : width + 128].astype(F32)[CAP:, :1] for i in range(n)], axis=0
-        )
-        g_acc[...] = jnp.zeros_like(g_acc)
-        u_acc[...] = jnp.zeros_like(u_acc)
+        share = sh_col[rows, :1]
+        gu_acc[...] = jnp.zeros_like(gu_acc)
         r_acc[...] = jnp.zeros_like(r_acc)
 
         def forward(b):
             cols = pl.ds(pl.multiple_of(b * kb, kb), kb)
-            tiles = [recv[g * n + i, :, cols].astype(F32) for i in range(n)]
+            tiles = [recv[g, b, i].astype(F32) for i in range(n)]
             zb = jnp.concatenate([t[:CAP] for t in tiles], axis=0).astype(BF16)
             dyf = jnp.concatenate([t[CAP:] for t in tiles], axis=0)
             rows_z[rows, cols] = zb
             rows_wdy[rows, cols] = (share * dyf).astype(BF16)
-            g_acc[...] += dot(zb, jnp.concatenate([w_gate[0, cols, :], w_gate[1, cols, :]], axis=1))
-            u_acc[...] += dot(zb, jnp.concatenate([w_up[0, cols, :], w_up[1, cols, :]], axis=1))
+            w_gu = [w_gate[0, cols, :], w_gate[1, cols, :], w_up[0, cols, :], w_up[1, cols, :]]
+            gu_acc[...] += dot(zb, jnp.concatenate(w_gu, axis=1))
             wd = jnp.concatenate([w_down[0, :, cols], w_down[1, :, cols]], axis=0)
             r_acc[...] += dot(dyf.astype(BF16), wd, NT)
 
         loop(0, nb, forward)
-        gv, uv, rv = g_acc[...], u_acc[...], r_acc[...]
+        gv, uv, rv = gu_acc[:, : 2 * hidden], gu_acc[:, 2 * hidden :], r_acc[...]
         sig = jax.nn.sigmoid(gv)
         act = gv * sig
         hv = act * uv
@@ -317,34 +397,30 @@
         )
         hid[rows, :] = hv.astype(BF16)
 
-        def backward(step):
-            dest = lax.rem(z + step, zn)
-            wrows = pl.ds(pl.multiple_of(dest * cols_z, cols_z), cols_z)
-            wg = jnp.concatenate([w_gate[0, wrows, :], w_gate[1, wrows, :]], axis=1)
-            wu = jnp.concatenate([w_up[0, wrows, :], w_up[1, wrows, :]], axis=1)
-            part = (dot(dg, wg, NT) + dot(du, wu, NT)).astype(BF16)
-
-            @pl.when(step > 0)
-            def _():
-                t_send[g, step] = part
-                t_copy(g, step).start()
-
-            @pl.when(step == 0)
-            def _():
-                t_recv[g, 0] = part
-
-        loop(0, zn, lambda i: backward(zn - 1 - i))
+        def backward(r):
+            wrows = pl.ds(pl.multiple_of(r * kb, kb), kb)
+            w_gu = [w_gate[0, wrows, :], w_up[0, wrows, :], w_gate[1, wrows, :], w_up[1, wrows, :]]
+            return dot(d_gu[rows, :], jnp.concatenate(w_gu, axis=1), NT)
+
+        for i in range(5):
+            t_send[g, i] = backward(plane(-turn(g) * ROLE[i])).astype(BF16)
+            near_copy(g, i).start()
+        for c in range(3):
+            t_own[g, c] = backward(own_class(g, c))
 
     def group_step(g):
         compute_group(g)
 
         @pl.when(g > 0)
         def _():
-            reduce_group(g - 1)
+            near_sums(g - 1)
+
+        @pl.when(g > 1)
+        def _():
+            far_sums(g - 2)
 
     loop(0, n, group_step)
 
-    nt = hr.shape[0] // 128
     term_own[...] = jnp.zeros_like(term_own)
     for i in range(nt):
         tile = hr[128 * i : 128 * (i + 1), :]
@@ -362,7 +438,10 @@
         dn_send[b] = dn[hidden:].astype(BF16)
         dn_copy(b).start()
 
-    loop(0, nb // 2, weight_grads)
+    loop(0, nb // 4, weight_grads)
+    near_sums(n - 1)
+    far_sums(n - 2)
+    loop(nb // 4, nb // 2, weight_grads)
     loop(1, zn, lambda j: tz_copy(j).wait_recv())
     total = term_own[...]
     for j in range(1, zn):
@@ -371,12 +450,7 @@
     loop(1, slots, lambda k: tb_copy(k).start())
     loop(nb // 2, nb, weight_grads)
     loop(1, slots, lambda k: tb_copy(k).wait_recv())
-    flat = lax.broadcasted_iota(jnp.int32, (8, 128), 0) * 128 + lax.broadcasted_iota(
-        jnp.int32, (8, 128), 1
-    )
-    terms = jnp.where(flat < CAP, term_sum[...], 0.0)
-    for k in range(1, slots):
-        terms = jnp.where((flat >= k * CAP) & (flat < (k + 1) * CAP), term_b[k], terms)
+    terms = merge(term_sum[...], term_b)
     term_row = jnp.concatenate([terms[i : i + 1] for i in range(nt)], axis=1)[:, : slots * CAP]
     choice = [jnp.sum(p * term_row, axis=1, keepdims=True) for p in places]
     mean_grad = shares[0] * choice[0] + shares[1] * choice[1]
@@ -390,7 +464,7 @@
     prod = dot(jnp.concatenate(parts, axis=0).astype(BF16), mod[:, my_cols])
     rc_own[...] = prod[:16] + prod[16:32] + prod[32:]
     rc_copy().start()
-    reduce_group(n - 1)
+    far_sums(n - 1)
 
     def finish(b):
         gu_copy(b).wait_recv()
@@ -416,7 +490,7 @@
     loop(nb // 2, nb, finish)
 
     def mod_part(i):
-        return dot(split3(logit_grad)[i][:, :experts], router[my_cols, :], NT)
+        return dot(split3(logit_grad)[i][:, :experts], router[:, my_cols])
 
     mod_grad = mod_part(0) + mod_part(1) + mod_part(2)
     gain = 1.0 + scale[:, my_cols]
@@ -455,11 +529,33 @@
     input_out[...] = inv_std * (norm_grad - total[:, 0:1] - normed * total[:, 1:2])
 
     def drain_slot(k):
-        send_copy(k).wait_send()
+        sh_copy(k).wait_send()
         b_copy(k).wait_send()
         tb_copy(k).wait_send()
 
+        @pl.when(k < RELAYED * n)
+        def _():
+            for c in range(3):
+                part_copy(k, c).wait_send()
+
+        @pl.when(k >= RELAYED * n)
+        def _():
+            direct_copy(k).wait_send()
+
     loop(1, slots, drain_slot)
+
+    def drain_group(g):
+        for i in range(5):
+            near_copy(g, i).wait_send()
+        for c in (1, 2):
+            far_copy(g, c).wait_send()
+
+        @pl.when(g < RELAYED)
+        def _():
+            for i in range(5):
+                relay_copy(g, i, own_class(g, CLASS[i])).wait_send()
+
+    loop(0, n, drain_group)
 
     def drain_ring(j):
         rx_copy(j, cx).wait_send()
@@ -471,7 +567,6 @@
     def drain_z(j):
         tz_copy(j).wait_send()
         ns_copy(j).wait_send()
-        loop(0, n, lambda g: t_copy(g, j).wait_send())
 
     loop(1, zn, drain_z)
 
@@ -480,6 +575,29 @@
         dn_copy(b).wait_send()
 
     loop(0, nb, drain_b)
+
+
+def copy_kernel(count, *refs):
+    sems = refs[-1]
+    copies = [
+        pltpu.make_async_copy(refs[i], refs[count + i], sems.at[i]) for i in range(count)
+    ]
+    for copy in copies:
+        copy.start()
+    for copy in copies:
+        copy.wait()
+
+
+def place_results(arrays):
+    count = len(arrays)
+    any_spec = pl.BlockSpec(memory_space=pl.ANY)
+    return pl.pallas_call(
+        functools.partial(copy_kernel, count),
+        out_shape=tuple(jax.ShapeDtypeStruct(a.shape, a.dtype) for a in arrays),
+        in_specs=[any_spec] * count,
+        out_specs=(any_spec,) * count,
+        scratch_shapes=[pltpu.SemaphoreType.DMA((count,))],
+    )(*arrays)
 
 
 def shards(
@@ -501,17 +619,18 @@
     experts = router_weight.shape[1]
     hidden = gate_blocks.shape[2]
     rows = slots * CAP
-    cols_z = width // zn
-    nb = width // 512
+    cols_z = kb = width // zn
+    nb = zn
     nt = -(-rows // 128)
+    group = n * CAP
     dma = pltpu.SemaphoreType.DMA
     vm = pltpu.VMEM
     scratch = [
         vm((toks, width), BF16),
         vm((toks, width), BF16),
         vm((rows, toks), BF16),
-        vm((slots, 2 * CAP, width + 128), BF16),
-        vm((slots, 2 * CAP, width + 128), BF16),
+        vm((slots, nb, 2 * CAP, kb), BF16),
+        vm((n, nb, n, 2 * CAP, kb), BF16),
         vm((2, width, hidden), BF16),
         vm((2, width, hidden), BF16),
         vm((2, hidden, width), BF16),
@@ -520,23 +639,28 @@
         vm((rows, 4 * hidden), BF16),
         vm((rows, 2 * hidden), BF16),
         vm((nt * 128, hidden), F32),
-        vm((n * CAP, 2 * hidden), F32),
-        vm((n * CAP, 2 * hidden), F32),
-        vm((n * CAP, 2 * hidden), F32),
-        vm((n, zn, n * CAP, cols_z), BF16),
-        vm((n, zn, n * CAP, cols_z), BF16),
-        vm((slots, 2 * CAP, cols_z // 2), BF16),
-        vm((slots, 2 * CAP, cols_z // 2), BF16),
+        vm((group, 4 * hidden), F32),
+        vm((group, 2 * hidden), F32),
+        vm((n, 5, group, kb), BF16),
+        vm((n, 5, group, kb), BF16),
+        vm((n, 3, group, kb), F32),
+        vm((n, 2, group, kb), BF16),
+        vm((n, 2, group, kb), BF16),
+        vm((slots, 2 * CAP, kb // 2), BF16),
+        vm((slots, 2 * CAP, kb // 2), BF16),
         vm((8, 128), F32),
         vm((zn, 8, 128), F32),
         vm((8, 128), F32),
         vm((slots, 8, 128), F32),
-        vm((nb, 512, 2 * hidden), F32),
-        vm((nb, 512, 2 * hidden), BF16),
-        vm((nb, 512, 2 * hidden), BF16),
-        vm((nb, hidden, 512), F32),
-        vm((nb, hidden, 512), BF16),
-        vm((nb, hidden, 512), BF16),
+        vm((8, 128), F32),
+        vm((slots, 8, 128), F32),
+        vm((nt * 128, 128), F32),
+        vm((nb, kb, 2 * hidden), F32),
+        vm((nb, kb, 2 * hidden), BF16),
+        vm((nb, kb, 2 * hidden), BF16),
+        vm((nb, hidden, kb), F32),
+        vm((nb, hidden, kb), BF16),
+        vm((nb, hidden, kb), BF16),
         vm((toks, 128), F32),
         vm((16, cols_z), F32),
         vm((16, cols_z), F32),
@@ -547,14 +671,15 @@
         vm((8, toks), F32),
         vm((zn, 8, toks), F32),
     ]
-    sems = [3, 3, 3, slots, slots, (n, zn), (n, zn), slots, slots]
+    sems = [3, 3, 3, (slots, 3), (slots, 3), (n, 5), (n, 5), (n, 5), (n, 5)]
+    sems += [(n, 2), (n, 2), slots, slots, slots, slots]
     sems += [zn, zn, slots, slots, nb, nb, nb, nb]
     sems += [1, 1, n, n, n, n, zn, zn]
     scratch += [dma(s if isinstance(s, tuple) else (s,)) for s in sems]
     any_spec = pl.BlockSpec(memory_space=pl.ANY)
     vm_spec = pl.BlockSpec(memory_space=pltpu.VMEM)
     row = lambda v: v.reshape(1, width)
-    grad_input, router_t, grad_gate, grad_up, grad_down = pl.pallas_call(
+    results = pl.pallas_call(
         functools.partial(expert_kernel, n, zn),
         out_shape=(
             jax.ShapeDtypeStruct((toks, cols_z), F32),
@@ -575,15 +700,16 @@
     )(
         tokens,
         cotangent,
-        expert_ids,
+        expert_ids.T,
         row(ada_shift),
         row(ada_scale),
         row(ada_gate),
-        router_weight,
+        router_weight.T,
         gate_blocks,
         up_blocks,
         down_blocks,
     )
+    grad_input, router_t, grad_gate, grad_up, grad_down = place_results(results)
     return (grad_input, router_t[:experts].T, grad_gate, grad_up, grad_down)
 
 

time: 166 us -> 221 us (1.33)
  Pallas kernels: 153 us -> 219 us
  local copies, waits for them, and re-layouts: 10.9 us -> 0 us
    pallas_call x0 -> x1, Pallas kernels: none -> 105 us  [place_results(): pl.pallas_call(functools.partial(copy_kernel, count), out_shape=tuple((ja...]
    pallas_call x1, Pallas kernels: 153 us -> 114 us  [shards(): pl.pallas_call(functools.partial(expert_kernel, n, zn), out_shape=(jax.Sh...]
    unnamed x15 -> x0, local copies, waits for them, and re-layouts: 10.9 us -> none
where the time goes in v3:
time: 221 us; the launch traced here: 220 us
  Pallas kernels  219 us (99%)
    pallas_call x1, Pallas kernels, shards(): pl.pallas_call(functools.partial(expert_kernel, n, zn), out_shape=(jax.Sh...  114 us
    pallas_call x1, Pallas kernels, place_results(): pl.pallas_call(functools.partial(copy_kernel, count), out_shape=tuple((ja...  105 us

profile of v3, /device:TPU:32, one launch (start us, length us, event | category | flops | bytes accessed | tf_op | source)
XLA Modules:
  0.0 219.7 jit_solution(1410911933928230507)
XLA Ops:
  0.6 113.7 %shard_map.137 = (f32[128,512]{1,0:T(8,128)}, f32[16,512]{1,0:T(8,128)}, bf16[1,4096,128]{2,1,0:T(8,128)(2,1)}, bf16[1,4096,128]{2,1,0:T(8,128)(2,1)}, bf16[1,128,4096]{2,1,0:T(8,128)(2,1)}) custom-call(bf16[128,4096]{1,0:T(8,128)(2,1)} %refs_0_.1, bf16[128,4096]{1,0:T(8,128)(2,1)} %refs_1_.1, s32[2,128]{1,0:T(2,128)} %bitcast.11, f32[1,4096]{1,0:T(1,128)} %bitcast.8, ...), custom_call_target="tpu_custom_call" | custom-call | flops 6442450944 | bytes 16777216 | tf_op jit(solution)/shard_map/pallas_call | solution.py:682
  114.4 105.4 %shard_map.138 = (f32[128,512]{1,0:T(8,128)}, f32[16,512]{1,0:T(8,128)}, bf16[1,4096,128]{2,1,0:T(8,128)(2,1)}, bf16[1,4096,128]{2,1,0:T(8,128)(2,1)}, bf16[1,128,4096]{2,1,0:T(8,128)(2,1)}) custom-call(f32[128,512]{1,0:T(8,128)} %get-tuple-element.15.refs_0_, f32[16,512]{1,0:T(8,128)} %get-tuple-element.16.refs_1_, ...), custom_call_target="tpu_custom_call" | custom-call | tf_op jit(solution)/shard_map/pallas_call | solution.py:594

commit v4 on v3

--- a/solution.py
+++ b/solution.py
@@ -579,12 +579,17 @@
 
 def copy_kernel(count, *refs):
     sems = refs[-1]
-    copies = [
-        pltpu.make_async_copy(refs[i], refs[count + i], sems.at[i]) for i in range(count)
+    held = refs[2 * count : 3 * count]
+    arrive = [pltpu.make_async_copy(refs[i], held[i], sems.at[0, i]) for i in range(count)]
+    leave = [
+        pltpu.make_async_copy(held[i], refs[count + i], sems.at[1, i]) for i in range(count)
     ]
-    for copy in copies:
+    for copy in arrive:
         copy.start()
-    for copy in copies:
+    for i in range(count):
+        arrive[i].wait()
+        leave[i].start()
+    for copy in leave:
         copy.wait()
 
 
@@ -596,7 +601,9 @@
         out_shape=tuple(jax.ShapeDtypeStruct(a.shape, a.dtype) for a in arrays),
         in_specs=[any_spec] * count,
         out_specs=(any_spec,) * count,
-        scratch_shapes=[pltpu.SemaphoreType.DMA((count,))],
+        scratch_shapes=[pltpu.VMEM(a.shape, a.dtype) for a in arrays]
+        + [pltpu.SemaphoreType.DMA((2, count))],
+        compiler_params=pltpu.CompilerParams(vmem_limit_bytes=16 * 1024 * 1024),
     )(*arrays)
 
 

time: 221 us -> 124 us (0.56)
  Pallas kernels: 219 us -> 116 us
  local copies, waits for them, and re-layouts: 0 us -> 5.37 us
    pallas_call x1, Pallas kernels: 105 us -> 2.11 us  [place_results(): pl.pallas_call(functools.partial(copy_kernel, count), out_shape=tuple((ja...]
    unnamed x0 -> x10, local copies, waits for them, and re-layouts: none -> 5.37 us
where the time goes in v4:
time: 124 us; the launch traced here: 122 us
  Pallas kernels  116 us (94%)
  local copies, waits for them, and re-layouts  5.37 us (4%)
    pallas_call x1, Pallas kernels, shards(): pl.pallas_call(functools.partial(expert_kernel, n, zn), out_shape=(jax.Sh...  114 us
    unnamed x10, local copies, waits for them, and re-layouts  5.37 us

profile of v4, /device:TPU:32, one launch (start us, length us, event | category | flops | bytes accessed | tf_op | source)
XLA Modules:
  0.0 121.9 jit_solution(7820671337611317454)
XLA Ops:
  0.6 113.7 %shard_map.137 = (f32[128,512]{1,0:T(8,128)}, f32[16,512]{1,0:T(8,128)}, bf16[1,4096,128]{2,1,0:T(8,128)(2,1)}, bf16[1,4096,128]{2,1,0:T(8,128)(2,1)}, bf16[1,128,4096]{2,1,0:T(8,128)(2,1)}) custom-call(bf16[128,4096]{1,0:T(8,128)(2,1)} %refs_0_.1, bf16[128,4096]{1,0:T(8,128)(2,1)} %refs_1_.1, s32[2,128]{1,0:T(2,128)} %bitcast.11, f32[1,4096]{1,0:T(1,128)} %bitcast.8, ...), custom_call_target="tpu_custom_call" | custom-call | flops 6442450944 | bytes 16777216 | tf_op jit(solution)/shard_map/pallas_call | solution.py:689
  114.4 0.0 copy-start
  114.4 1.2 copy-done
  115.6 0.0 copy-start.1
  115.6 1.2 %copy-done.1 = bf16[1,4096,128]{2,1,0:T(8,128)(2,1)S(1)} copy-done((bf16[1,4096,128]{2,1,0:T(8,128)(2,1)S(1)}, bf16[1,4096,128]{2,1,0:T(8,128)(2,1)}, u32[]{:S(2)}) %copy-start.1) | copy-done | bytes 1048600
  116.8 0.0 copy-start.2
  116.8 1.2 %copy-done.2 = bf16[1,128,4096]{2,1,0:T(8,128)(2,1)S(1)} copy-done((bf16[1,128,4096]{2,1,0:T(8,128)(2,1)S(1)}, bf16[1,128,4096]{2,1,0:T(8,128)(2,1)}, u32[]{:S(2)}) %copy-start.2) | copy-done | bytes 1048600
  118.1 0.0 copy-start.3
  118.1 0.9 copy-done.3
  119.0 0.0 copy-start.4
  119.0 0.8 copy-done.4
  119.8 2.1 %shard_map.138 = (f32[128,512]{1,0:T(8,128)}, f32[16,512]{1,0:T(8,128)}, bf16[1,4096,128]{2,1,0:T(8,128)(2,1)}, bf16[1,4096,128]{2,1,0:T(8,128)(2,1)}, bf16[1,128,4096]{2,1,0:T(8,128)(2,1)}) custom-call(f32[128,512]{1,0:T(8,128)S(1)} %copy-done.3, f32[16,512]{1,0:T(8,128)S(1)} %copy-done.4, bf16[1,4096,128]{2,1,0:T(8,128)(2,1)S(1)} %copy-done, ...), custom_call_target="tpu_custom_call" | custom-call | tf_op jit(solution)/shard_map/pallas_call | solution.py:599
Async XLA Ops:
  114.4 1.2 %copy-start = (bf16[1,4096,128]{2,1,0:T(8,128)(2,1)S(1)}, bf16[1,4096,128]{2,1,0:T(8,128)(2,1)}, u32[]{:S(2)}) copy-start(bf16[1,4096,128]{2,1,0:T(8,128)(2,1)} %get-tuple-element.17.refs_2_) | copy-start | bytes 3145732
  115.6 1.2 %copy-start.1 = (bf16[1,4096,128]{2,1,0:T(8,128)(2,1)S(1)}, bf16[1,4096,128]{2,1,0:T(8,128)(2,1)}, u32[]{:S(2)}) copy-start(bf16[1,4096,128]{2,1,0:T(8,128)(2,1)} %get-tuple-element.18.refs_3_) | copy-start | bytes 3145732
  116.8 1.2 %copy-start.2 = (bf16[1,128,4096]{2,1,0:T(8,128)(2,1)S(1)}, bf16[1,128,4096]{2,1,0:T(8,128)(2,1)}, u32[]{:S(2)}) copy-start(bf16[1,128,4096]{2,1,0:T(8,128)(2,1)} %get-tuple-element.19.refs_4_) | copy-start | bytes 3145732
  118.1 0.9 copy-start.3
  119.0 0.8 copy-start.4

commit v5 on v4

--- a/solution.py
+++ b/solution.py
@@ -45,15 +45,15 @@
         (tokens, cotangent, ids, shift, scale, ada_gate, router, gate, up, down),
         (input_out, router_out, gate_out, up_out, down_out),
         (mod, og, place_t, send, recv, w_gate, w_up, w_down, rows_z, rows_wdy, d_gu, hid, hr),
-        (gu_acc, r_acc, t_send, t_in, t_own, m_send, m_in, b_send, b_recv),
+        (gu_acc, r_acc, t_send, t_in, t_own, m_send, m_in, b_send, b_recv, e_acc),
         (term_own, term_z, term_sum, term_b, sh_own, sh_recv, sh_col),
         (gu_own, gu_send, gu_recv, dn_own, dn_send, dn_recv),
-        (logit_acc, rc_own, rc_sib, rx_sum, rx_buf, ry_sum, ry_buf, ns_own, ns_z),
+        (logit_acc, stat, rc_own, rc_sib, rx_sum, rx_buf, ry_sum, ry_buf, ns_own, ns_z),
         (w_local, w_ssem, w_rsem, d_ssem, d_rsem, f_ssem, f_rsem, a_ssem, a_rsem),
         (m_ssem, m_rsem, b_ssem, b_rsem, sh_ssem, sh_rsem),
         (tz_ssem, tz_rsem, tb_ssem, tb_rsem, g_ssem, g_rsem, h_ssem, h_rsem),
         (rc_ssem, rc_rsem, rx_ssem, rx_rsem, ry_ssem, ry_rsem, ns_ssem, ns_rsem),
-    ) = split_refs(refs, (10, 5, 13, 9, 7, 6, 9, 9, 6, 8, 8))
+    ) = split_refs(refs, (10, 5, 13, 10, 7, 6, 10, 9, 6, 8, 8))
     slots = n * n
     width = rows_z.shape[1]
     group = n * CAP
@@ -94,11 +94,10 @@
     def plane(step):
         return lax.rem(z + step + 2 * zn, zn)
 
-    def turn(g):
-        return 1 - 2 * lax.rem(g, 2)
-
-    def own_class(g, c):
-        return plane(-3 * turn(g) * c)
+    turn = 1 - 2 * core
+
+    def own_class(c):
+        return plane(-3 * turn * c)
 
     def direct_copy(slot):
         dst = recv.at[slot // n, :, lax.rem(slot, n)]
@@ -106,21 +105,21 @@
 
     def part_copy(slot, c):
         g = slot // n
-        r = own_class(g, c)
+        r = own_class(c)
         dst = recv.at[g, r, lax.rem(slot, n)]
         return remote(send.at[slot, r], dst, d_ssem.at[slot, c], d_rsem.at[slot, c], target(slot))
 
     def relay_copy(g, i, r):
-        to = (seq, plane(turn(g) * SIGN[i]))
+        to = (seq, plane(turn * SIGN[i]))
         return remote(recv.at[g, r], recv.at[g, r], f_ssem.at[g, i], f_rsem.at[g, i], to)
 
     def near_copy(g, i):
-        to = (seq, plane(-turn(g) * SIGN[i]))
+        to = (seq, plane(-turn * SIGN[i]))
         return remote(t_send.at[g, i], t_in.at[g, i], a_ssem.at[g, i], a_rsem.at[g, i], to)
 
-    def far_copy(g, c):
-        to = (seq, own_class(g, c))
-        return remote(m_send.at[g, c - 1], m_in.at[g, c - 1], m_ssem.at[g, c - 1], m_rsem.at[g, c - 1], to)
+    def far_copy(c):
+        to = (seq, own_class(c))
+        return remote(m_send.at[c - 1], m_in.at[c - 1], m_ssem.at[c - 1], m_rsem.at[c - 1], to)
 
     def sh_copy(slot):
         return remote(sh_own, sh_recv.at[slot], sh_ssem.at[slot], sh_rsem.at[slot], target(slot))
@@ -186,38 +185,10 @@
     for i in range(3):
         w_copy_local(i).start()
 
-    def moment(center):
-        def body(b, acc):
-            cols = pl.ds(pl.multiple_of(b * kb, kb), kb)
-            x = tokens[:, cols].astype(F32)
-            if center is not None:
-                x = (x - center) * (x - center)
-            return acc + jnp.sum(x, axis=1, keepdims=True)
-
-        return lax.fori_loop(0, nb, body, jnp.zeros((toks, 1), F32)) * (1.0 / width)
-
-    mean = moment(None)
-    inv_std = lax.rsqrt(moment(mean) + EPSILON)
-    logit_acc[...] = jnp.zeros_like(logit_acc)
     experts = router.shape[0]
-
-    def modulate(b):
-        cols = pl.ds(pl.multiple_of(b * kb, kb), kb)
-        normed = (tokens[:, cols].astype(F32) - mean) * inv_std
-        m = (normed * (1.0 + scale[:, cols]) + shift[:, cols]).astype(BF16)
-        mod[:, cols] = m
-        og[:, cols] = (ada_gate[:, cols] * cotangent[:, cols].astype(F32)).astype(BF16)
-        logit_acc[:, :experts] += dot(m, router[:, cols], NT)
-
-    loop(0, nb, modulate)
-    scores = jax.nn.sigmoid(logit_acc[...])
     expert_at = lax.broadcasted_iota(jnp.int32, (toks, 128), 1)
     ids_t = jnp.concatenate([ids[...].astype(F32), jnp.zeros((126, toks), F32)], axis=0).T
     hits = [expert_at.astype(F32) == ids_t[:, k : k + 1] for k in range(2)]
-    picked = [jnp.sum(jnp.where(h, scores, 0.0), axis=1, keepdims=True) for h in hits]
-    score_sum = picked[0] + picked[1]
-    shares = [p / score_sum for p in picked]
-    share_r = [s.astype(BF16).astype(F32) for s in shares]
     routed = jnp.where(hits[0] | hits[1], 1.0, 0.0)
     tok_at = lax.broadcasted_iota(jnp.int32, (toks, toks), 0)
     earlier = jnp.where(tok_at > lax.broadcasted_iota(jnp.int32, (toks, toks), 1), 1.0, 0.0)
@@ -243,6 +214,75 @@
             out = jnp.where((flat >= k * CAP) & (flat < (k + 1) * CAP), others[k], out)
         return out
 
+    def modulate(i):
+        rows = pl.ds(pl.multiple_of(i * 16, 16), 16)
+        x = tokens[rows, :].astype(F32)
+        center = jnp.sum(x, axis=1, keepdims=True) * (1.0 / width)
+        x = x - center
+        inv = lax.rsqrt(jnp.sum(x * x, axis=1, keepdims=True) * (1.0 / width) + EPSILON)
+        mod[rows, :] = (x * inv * (1.0 + scale[...]) + shift[...]).astype(BF16)
+        og[rows, :] = (ada_gate[...] * cotangent[rows, :].astype(F32)).astype(BF16)
+        stat[rows, :] = jnp.where(lax.broadcasted_iota(jnp.int32, (16, 128), 1) == 0, center, inv)
+
+    loop(0, toks // 16, modulate)
+    mean, inv_std = stat[:, 0:1], stat[:, 1:2]
+    hr[...] = jnp.zeros_like(hr)
+    pl.semaphore_wait(barrier, slots + zn - 1)
+    for i in range(3):
+        w_copy(i).start()
+
+    def fill(g, b):
+        rows = pl.ds(pl.multiple_of(g * group, group), group)
+        cols = pl.ds(pl.multiple_of(b * kb, kb), kb)
+        zc = dot(place_t[rows, :], mod[:, cols])
+        dc = dot(place_t[rows, :], og[:, cols])
+        for i in range(n):
+            at = slice(i * CAP, (i + 1) * CAP)
+            pair = jnp.concatenate([zc[at], dc[at]], axis=0).astype(BF16)
+
+            @pl.when(g * n + i > 0)
+            def _():
+                send[g * n + i, b] = pair
+
+            if i == 0:
+
+                @pl.when(g == 0)
+                def _():
+                    recv[0, b, 0] = pair
+
+    def each_remote(g, body):
+        def one(i):
+            @pl.when(g * n + i > 0)
+            def _():
+                body(g * n + i)
+
+        loop(0, n, one)
+
+    def relayed_start(g):
+        for c in range(3):
+            fill(g, own_class(c))
+            each_remote(g, lambda slot: part_copy(slot, c).start())
+
+    def relayed_arrive(g):
+        for c in range(3):
+            each_remote(g, lambda slot: part_copy(slot, c).wait_recv())
+            for i in range(5):
+                if CLASS[i] == c:
+                    relay_copy(g, i, own_class(c)).start()
+
+    relayed_start(0)
+    logit_acc[...] = jnp.zeros_like(logit_acc)
+
+    def add_logits(b):
+        cols = pl.ds(pl.multiple_of(b * kb, kb), kb)
+        logit_acc[:, :experts] += dot(mod[:, cols], router[:, cols], NT)
+
+    loop(0, nb, add_logits)
+    scores = jax.nn.sigmoid(logit_acc[...])
+    picked = [jnp.sum(jnp.where(h, scores, 0.0), axis=1, keepdims=True) for h in hits]
+    score_sum = picked[0] + picked[1]
+    shares = [p / score_sum for p in picked]
+    share_r = [s.astype(BF16).astype(F32) for s in shares]
     share_row = jnp.sum(places[0] * share_r[0] + places[1] * share_r[1], axis=0, keepdims=True)
     if nt * 128 > slots * CAP:
         share_row = jnp.concatenate(
@@ -251,54 +291,8 @@
     sh_own[...] = jnp.zeros_like(sh_own)
     for i in range(nt):
         sh_own[i : i + 1, :] = share_row[:, 128 * i : 128 * (i + 1)]
-
-    hr[...] = jnp.zeros_like(hr)
-    pl.semaphore_wait(barrier, slots + zn - 1)
-    for i in range(3):
-        w_copy(i).start()
-
     loop(1, slots, lambda k: sh_copy(k).start())
-
-    def fill(g, b):
-        rows = pl.ds(pl.multiple_of(g * group, group), group)
-        cols = pl.ds(pl.multiple_of(b * kb, kb), kb)
-        zc = dot(place_t[rows, :], mod[:, cols])
-        dc = dot(place_t[rows, :], og[:, cols])
-        for i in range(n):
-            at = slice(i * CAP, (i + 1) * CAP)
-            pair = jnp.concatenate([zc[at], dc[at]], axis=0).astype(BF16)
-
-            @pl.when(g * n + i > 0)
-            def _():
-                send[g * n + i, b] = pair
-
-            if i == 0:
-
-                @pl.when(g == 0)
-                def _():
-                    recv[0, b, 0] = pair
-
-    def each_remote(g, body):
-        def one(i):
-            @pl.when(g * n + i > 0)
-            def _():
-                body(g * n + i)
-
-        loop(0, n, one)
-
-    def relayed_start(g):
-        for c in range(3):
-            fill(g, own_class(g, c))
-            each_remote(g, lambda slot: part_copy(slot, c).start())
-
-    def relayed_arrive(g):
-        for c in range(3):
-            each_remote(g, lambda slot: part_copy(slot, c).wait_recv())
-            for i in range(5):
-                if CLASS[i] == c:
-                    relay_copy(g, i, own_class(g, c)).start()
-
-    loop(0, RELAYED, relayed_start)
+    loop(1, RELAYED, relayed_start)
     loop(RELAYED, n, lambda g: loop(0, nb, lambda b: fill(g, b)))
     for g in range(RELAYED):
         relayed_arrive(g)
@@ -317,7 +311,7 @@
         @pl.when(g < RELAYED)
         def _():
             for i in range(5):
-                relay_copy(g, i, plane(-turn(g) * ROLE[i])).wait_recv()
+                relay_copy(g, i, plane(-turn * ROLE[i])).wait_recv()
 
         @pl.when(g >= RELAYED)
         def _():
@@ -330,38 +324,46 @@
     def near_sums(g):
         for i in range(5):
             near_copy(g, i).wait_recv()
-        for c in (1, 2, 0):
+        packed = []
+        for c in range(3):
             total = t_own[g, c]
             for i in range(5):
                 if CLASS[i] == c:
                     total = total + t_in[g, i].astype(F32)
-            if c > 0:
-                m_send[g, c - 1] = total.astype(BF16)
-                far_copy(g, c).start()
-            else:
-                t_own[g, 0] = total
-
-    def far_sums(g):
-        for c in (1, 2):
-            far_copy(g, c).wait_recv()
-        total = t_own[g, 0] + m_in[g, 0].astype(F32) + m_in[g, 1].astype(F32)
+            packed.append(total)
         for i in range(n):
             slot = g * n + i
-            part = total[i * CAP : (i + 1) * CAP]
-            packed = jnp.concatenate([part[:, :half], part[:, half:]], axis=0).astype(BF16)
-            if i > 0:
-                b_send[slot] = packed
+            at = slice(i * CAP, (i + 1) * CAP)
+            folded = [
+                jnp.concatenate([t[at, :half], t[at, half:]], axis=0).astype(BF16) for t in packed
+            ]
+
+            @pl.when(slot > 0)
+            def _():
+                for c in range(3):
+                    b_send[slot, c] = folded[c]
                 b_copy(slot).start()
-            else:
-
-                @pl.when(slot > 0)
-                def _():
-                    b_send[slot] = packed
-                    b_copy(slot).start()
+
+            if i == 0:
 
                 @pl.when(slot == 0)
                 def _():
-                    b_recv[0] = packed
+                    for c in range(3):
+                        b_recv[0, c] = folded[c]
+
+    def combine(g):
+        loop(
+            0,
+            n,
+            lambda i: pl.when(g * n + i > 0)(lambda: b_copy(g * n + i).wait_recv()),
+        )
+        rows = pl.ds(pl.multiple_of(g * group, group), group)
+        for c in range(3):
+            tiles = [b_recv[g * n + i, c].astype(F32) for i in range(n)]
+            low = jnp.concatenate([t[:CAP] for t in tiles], axis=0)
+            high = jnp.concatenate([t[CAP:] for t in tiles], axis=0)
+            back = jnp.concatenate([low, high], axis=1).astype(BF16)
+            e_acc[c] += dot(place_t[rows, :], back, TN)
 
     def compute_group(g):
         wait_group(g)
@@ -403,10 +405,10 @@
             return dot(d_gu[rows, :], jnp.concatenate(w_gu, axis=1), NT)
 
         for i in range(5):
-            t_send[g, i] = backward(plane(-turn(g) * ROLE[i])).astype(BF16)
+            t_send[g, i] = backward(plane(-turn * ROLE[i])).astype(BF16)
             near_copy(g, i).start()
         for c in range(3):
-            t_own[g, c] = backward(own_class(g, c))
+            t_own[g, c] = backward(own_class(c))
 
     def group_step(g):
         compute_group(g)
@@ -414,10 +416,6 @@
         @pl.when(g > 0)
         def _():
             near_sums(g - 1)
-
-        @pl.when(g > 1)
-        def _():
-            far_sums(g - 2)
 
     loop(0, n, group_step)
 
@@ -438,17 +436,17 @@
         dn_send[b] = dn[hidden:].astype(BF16)
         dn_copy(b).start()
 
-    loop(0, nb // 4, weight_grads)
-    near_sums(n - 1)
-    far_sums(n - 2)
-    loop(nb // 4, nb // 2, weight_grads)
+    loop(0, nb // 2, weight_grads)
     loop(1, zn, lambda j: tz_copy(j).wait_recv())
     total = term_own[...]
     for j in range(1, zn):
         total = total + term_z[j]
     term_sum[...] = total
     loop(1, slots, lambda k: tb_copy(k).start())
+    near_sums(n - 1)
     loop(nb // 2, nb, weight_grads)
+    e_acc[...] = jnp.zeros_like(e_acc)
+    loop(0, n - 1, combine)
     loop(1, slots, lambda k: tb_copy(k).wait_recv())
     terms = merge(term_sum[...], term_b)
     term_row = jnp.concatenate([terms[i : i + 1] for i in range(nt)], axis=1)[:, : slots * CAP]
@@ -464,7 +462,29 @@
     prod = dot(jnp.concatenate(parts, axis=0).astype(BF16), mod[:, my_cols])
     rc_own[...] = prod[:16] + prod[16:32] + prod[32:]
     rc_copy().start()
-    far_sums(n - 1)
+    lg_parts = split3(logit_grad)
+    mod_grad = sum(dot(p[:, :experts], router[:, my_cols]) for p in lg_parts)
+    combine(n - 1)
+    for c in (1, 2):
+        m_send[c - 1] = e_acc[c].astype(BF16)
+        far_copy(c).start()
+
+    def gain_normed(r):
+        cols = pl.ds(pl.multiple_of(r * kb, kb), kb)
+        return 1.0 + scale[:, cols], (tokens[:, cols].astype(F32) - mean) * inv_std
+
+    gain, normed = gain_normed(z)
+    sums = [jnp.zeros((toks, 1), F32)] * 2
+    for c in range(3):
+        gain_c, normed_c = gain_normed(own_class(c))
+        part = e_acc[c] if c > 0 else e_acc[0] + mod_grad
+        part = part * gain_c
+        sums[0] = sums[0] + jnp.sum(part, axis=1, keepdims=True)
+        sums[1] = sums[1] + jnp.sum(part * normed_c, axis=1, keepdims=True)
+    lane = lax.broadcasted_iota(jnp.int32, (toks, 128), 1)
+    sums_t = jnp.where(lane == 0, sums[0], jnp.where(lane == 1, sums[1], 0.0)).T
+    ns_own[...] = sums_t[:8]
+    loop(1, zn, lambda j: ns_copy(j).start())
 
     def finish(b):
         gu_copy(b).wait_recv()
@@ -489,32 +509,10 @@
     loop(1, n, lambda j: ry_copy(j, cy).start())
     loop(nb // 2, nb, finish)
 
-    def mod_part(i):
-        return dot(split3(logit_grad)[i][:, :experts], router[:, my_cols])
-
-    mod_grad = mod_part(0) + mod_part(1) + mod_part(2)
-    gain = 1.0 + scale[:, my_cols]
-    normed = (tokens[:, my_cols].astype(F32) - mean) * inv_std
-
-    loop(1, slots, lambda k: b_copy(k).wait_recv())
-    tiles = [b_recv[k].astype(F32) for k in range(slots)]
-    rows_back = jnp.concatenate(
-        [
-            jnp.concatenate([t[:CAP] for t in tiles], axis=0),
-            jnp.concatenate([t[CAP:] for t in tiles], axis=0),
-        ],
-        axis=1,
-    ).astype(BF16)
-    norm_grad = (mod_grad + dot(place_t[...], rows_back, TN)) * gain
-    sums = [
-        jnp.sum(norm_grad, axis=1, keepdims=True),
-        jnp.sum(norm_grad * normed, axis=1, keepdims=True),
-    ]
-    lane = lax.broadcasted_iota(jnp.int32, (toks, 128), 1)
-    sums_t = jnp.where(lane == 0, sums[0], jnp.where(lane == 1, sums[1], 0.0)).T
-    ns_own[...] = sums_t[:8]
-    loop(1, zn, lambda j: ns_copy(j).start())
-
+    for c in (1, 2):
+        far_copy(c).wait_recv()
+    expert_grad = e_acc[0] + m_in[0].astype(F32) + m_in[1].astype(F32)
+    norm_grad = (mod_grad + expert_grad) * gain
     loop(1, n, lambda j: ry_copy(j, lax.rem(cy + j, n)).wait_recv())
     total = ry_buf[0]
     for j in range(1, n):
@@ -547,15 +545,15 @@
     def drain_group(g):
         for i in range(5):
             near_copy(g, i).wait_send()
-        for c in (1, 2):
-            far_copy(g, c).wait_send()
 
         @pl.when(g < RELAYED)
         def _():
             for i in range(5):
-                relay_copy(g, i, own_class(g, CLASS[i])).wait_send()
+                relay_copy(g, i, own_class(CLASS[i])).wait_send()
 
     loop(0, n, drain_group)
+    for c in (1, 2):
+        far_copy(c).wait_send()
 
     def drain_ring(j):
         rx_copy(j, cx).wait_send()
@@ -603,7 +601,7 @@
         out_specs=(any_spec,) * count,
         scratch_shapes=[pltpu.VMEM(a.shape, a.dtype) for a in arrays]
         + [pltpu.SemaphoreType.DMA((2, count))],
-        compiler_params=pltpu.CompilerParams(vmem_limit_bytes=16 * 1024 * 1024),
+        compiler_params=pltpu.CompilerParams(vmem_limit_bytes=60 * 1024 * 1024),
     )(*arrays)
 
 
@@ -651,10 +649,11 @@
         vm((n, 5, group, kb), BF16),
         vm((n, 5, group, kb), BF16),
         vm((n, 3, group, kb), F32),
-        vm((n, 2, group, kb), BF16),
-        vm((n, 2, group, kb), BF16),
-        vm((slots, 2 * CAP, kb // 2), BF16),
-        vm((slots, 2 * CAP, kb // 2), BF16),
+        vm((2, toks, kb), BF16),
+        vm((2, toks, kb), BF16),
+        vm((slots, 3, 2 * CAP, kb // 2), BF16),
+        vm((slots, 3, 2 * CAP, kb // 2), BF16),
+        vm((3, toks, kb), F32),
         vm((8, 128), F32),
         vm((zn, 8, 128), F32),
         vm((8, 128), F32),
@@ -669,6 +668,7 @@
         vm((nb, hidden, kb), BF16),
         vm((nb, hidden, kb), BF16),
         vm((toks, 128), F32),
+        vm((toks, 128), F32),
         vm((16, cols_z), F32),
         vm((16, cols_z), F32),
         vm((16, cols_z), F32),
@@ -679,7 +679,7 @@
         vm((zn, 8, toks), F32),
     ]
     sems = [3, 3, 3, (slots, 3), (slots, 3), (n, 5), (n, 5), (n, 5), (n, 5)]
-    sems += [(n, 2), (n, 2), slots, slots, slots, slots]
+    sems += [2, 2, slots, slots, slots, slots]
     sems += [zn, zn, slots, slots, nb, nb, nb, nb]
     sems += [1, 1, n, n, n, n, zn, zn]
     scratch += [dma(s if isinstance(s, tuple) else (s,)) for s in sems]

time: 124 us -> 114 us (0.919)
  local copies, waits for them, and re-layouts: 5.37 us -> 0 us
  Pallas kernels: 116 us -> 111 us
    pallas_call x1, Pallas kernels: 114 us -> 108 us  [shards(): pl.pallas_call(functools.partial(expert_kernel, n, zn), out_shape=(jax.Sh...]
    unnamed x10 -> x0, local copies, waits for them, and re-layouts: 5.37 us -> none
where the time goes in v5:
time: 114 us; the launch traced here: 112 us
  Pallas kernels  111 us (97%)
    pallas_call x1, Pallas kernels, shards(): pl.pallas_call(functools.partial(expert_kernel, n, zn), out_shape=(jax.Sh...  108 us
    pallas_call x1, Pallas kernels, place_results(): pl.pallas_call(functools.partial(copy_kernel, count), out_shape=tuple((ja...  3.13 us

profile of v5, /device:TPU:32, one launch (start us, length us, event | category | flops | bytes accessed | tf_op | source)
XLA Modules:
  0.0 111.7 jit_solution(12707902809448840346)
XLA Ops:
  0.6 107.9 %shard_map.137 = (f32[128,512]{1,0:T(8,128)}, f32[16,512]{1,0:T(8,128)}, bf16[1,4096,128]{2,1,0:T(8,128)(2,1)}, bf16[1,4096,128]{2,1,0:T(8,128)(2,1)}, bf16[1,128,4096]{2,1,0:T(8,128)(2,1)}) custom-call(bf16[128,4096]{1,0:T(8,128)(2,1)} %refs_0_.1, bf16[128,4096]{1,0:T(8,128)(2,1)} %refs_1_.1, s32[2,128]{1,0:T(2,128)} %bitcast.11, f32[1,4096]{1,0:T(1,128)} %bitcast.8, ...), custom_call_target="tpu_custom_call" | custom-call | flops 6442450944 | bytes 16777216 | tf_op jit(solution)/shard_map/pallas_call | solution.py:689
  108.6 3.1 %shard_map.138 = (f32[128,512]{1,0:T(8,128)}, f32[16,512]{1,0:T(8,128)}, bf16[1,4096,128]{2,1,0:T(8,128)(2,1)}, bf16[1,4096,128]{2,1,0:T(8,128)(2,1)}, bf16[1,128,4096]{2,1,0:T(8,128)(2,1)}) custom-call(f32[128,512]{1,0:T(8,128)} %get-tuple-element.15.refs_0_, f32[16,512]{1,0:T(8,128)} %get-tuple-element.16.refs_1_, ...), custom_call_target="tpu_custom_call" | custom-call | tf_op jit(solution)/shard_map/pallas_call | solution.py:597

commit v6 on v5

--- a/solution.py
+++ b/solution.py
@@ -9,7 +9,7 @@
 from jax.sharding import PartitionSpec as P
 
 CAP = 24
-RELAYED = 2
+RELAYED = 3
 ROLE = (1, 7, 4, 2, 5)
 CLASS = (0, 0, 1, 1, 2)
 SIGN = (1, -1, 1, -1, -1)
@@ -124,8 +124,9 @@
     def sh_copy(slot):
         return remote(sh_own, sh_recv.at[slot], sh_ssem.at[slot], sh_rsem.at[slot], target(slot))
 
-    def b_copy(slot):
-        return remote(b_send.at[slot], b_recv.at[slot], b_ssem.at[slot], b_rsem.at[slot], source(slot))
+    def b_copy(slot, c):
+        src, dst = b_send.at[slot, c], b_recv.at[slot, c]
+        return remote(src, dst, b_ssem.at[slot, c], b_rsem.at[slot, c], source(slot))
 
     def tz_copy(step):
         return remote(term_own, term_z.at[step], tz_ssem.at[step], tz_rsem.at[step], z_peer(step))
@@ -322,48 +323,48 @@
             loop((RELAYED + 1) * n, slots, lambda k: direct_copy(k).start())
 
     def near_sums(g):
-        for i in range(5):
-            near_copy(g, i).wait_recv()
-        packed = []
-        for c in range(3):
+        for c in (1, 2, 0):
             total = t_own[g, c]
             for i in range(5):
                 if CLASS[i] == c:
+                    near_copy(g, i).wait_recv()
                     total = total + t_in[g, i].astype(F32)
-            packed.append(total)
-        for i in range(n):
-            slot = g * n + i
-            at = slice(i * CAP, (i + 1) * CAP)
-            folded = [
-                jnp.concatenate([t[at, :half], t[at, half:]], axis=0).astype(BF16) for t in packed
-            ]
-
-            @pl.when(slot > 0)
-            def _():
-                for c in range(3):
-                    b_send[slot, c] = folded[c]
-                b_copy(slot).start()
-
-            if i == 0:
-
-                @pl.when(slot == 0)
+            for i in range(n):
+                slot = g * n + i
+                at = slice(i * CAP, (i + 1) * CAP)
+                folded = jnp.concatenate([total[at, :half], total[at, half:]], axis=0)
+                folded = folded.astype(BF16)
+
+                @pl.when(slot > 0)
                 def _():
-                    for c in range(3):
-                        b_recv[0, c] = folded[c]
-
-    def combine(g):
+                    b_send[slot, c] = folded
+                    b_copy(slot, c).start()
+
+                if i == 0:
+
+                    @pl.when(slot == 0)
+                    def _():
+                        b_recv[0, c] = folded
+
+    def combine(g, c):
         loop(
             0,
             n,
-            lambda i: pl.when(g * n + i > 0)(lambda: b_copy(g * n + i).wait_recv()),
+            lambda i: pl.when(g * n + i > 0)(lambda: b_copy(g * n + i, c).wait_recv()),
         )
         rows = pl.ds(pl.multiple_of(g * group, group), group)
-        for c in range(3):
-            tiles = [b_recv[g * n + i, c].astype(F32) for i in range(n)]
-            low = jnp.concatenate([t[:CAP] for t in tiles], axis=0)
-            high = jnp.concatenate([t[CAP:] for t in tiles], axis=0)
-            back = jnp.concatenate([low, high], axis=1).astype(BF16)
-            e_acc[c] += dot(place_t[rows, :], back, TN)
+        tiles = [b_recv[g * n + i, c].astype(F32) for i in range(n)]
+        low = jnp.concatenate([t[:CAP] for t in tiles], axis=0)
+        high = jnp.concatenate([t[CAP:] for t in tiles], axis=0)
+        back = jnp.concatenate([low, high], axis=1).astype(BF16)
+        e_acc[c] += dot(place_t[rows, :], back, TN)
+
+    def send_terms():
+        term_own[...] = jnp.zeros_like(term_own)
+        for i in range(nt):
+            tile = hr[128 * i : 128 * (i + 1), :]
+            term_own[i : i + 1, :] = jnp.sum(tile.T, axis=0, keepdims=True)
+        loop(1, zn, lambda j: tz_copy(j).start())
 
     def compute_group(g):
         wait_group(g)
@@ -399,15 +400,19 @@
         )
         hid[rows, :] = hv.astype(BF16)
 
+        @pl.when(g == n - 1)
+        def _():
+            send_terms()
+
         def backward(r):
             wrows = pl.ds(pl.multiple_of(r * kb, kb), kb)
             w_gu = [w_gate[0, wrows, :], w_up[0, wrows, :], w_gate[1, wrows, :], w_up[1, wrows, :]]
             return dot(d_gu[rows, :], jnp.concatenate(w_gu, axis=1), NT)
 
-        for i in range(5):
+        for i in (2, 3, 4, 0, 1):
             t_send[g, i] = backward(plane(-turn * ROLE[i])).astype(BF16)
             near_copy(g, i).start()
-        for c in range(3):
+        for c in (1, 2, 0):
             t_own[g, c] = backward(own_class(c))
 
     def group_step(g):
@@ -418,12 +423,6 @@
             near_sums(g - 1)
 
     loop(0, n, group_step)
-
-    term_own[...] = jnp.zeros_like(term_own)
-    for i in range(nt):
-        tile = hr[128 * i : 128 * (i + 1), :]
-        term_own[i : i + 1, :] = jnp.sum(tile.T, axis=0, keepdims=True)
-    loop(1, zn, lambda j: tz_copy(j).start())
 
     def weight_grads(b):
         cols = pl.ds(pl.multiple_of(b * kb, kb), kb)
@@ -436,17 +435,28 @@
         dn_send[b] = dn[hidden:].astype(BF16)
         dn_copy(b).start()
 
-    loop(0, nb // 2, weight_grads)
+    first, last = nb // 4, nb * 5 // 8
+    loop(0, first, weight_grads)
+    near_sums(n - 1)
     loop(1, zn, lambda j: tz_copy(j).wait_recv())
     total = term_own[...]
     for j in range(1, zn):
         total = total + term_z[j]
     term_sum[...] = total
     loop(1, slots, lambda k: tb_copy(k).start())
-    near_sums(n - 1)
-    loop(nb // 2, nb, weight_grads)
     e_acc[...] = jnp.zeros_like(e_acc)
-    loop(0, n - 1, combine)
+
+    def combine_all(g):
+        for c in range(3):
+            combine(g, c)
+
+    loop(0, n - 1, combine_all)
+    loop(first, last, weight_grads)
+    for c in (1, 2):
+        combine(n - 1, c)
+        m_send[c - 1] = e_acc[c].astype(BF16)
+        far_copy(c).start()
+    combine(n - 1, 0)
     loop(1, slots, lambda k: tb_copy(k).wait_recv())
     terms = merge(term_sum[...], term_b)
     term_row = jnp.concatenate([terms[i : i + 1] for i in range(nt)], axis=1)[:, : slots * CAP]
@@ -464,11 +474,6 @@
     rc_copy().start()
     lg_parts = split3(logit_grad)
     mod_grad = sum(dot(p[:, :experts], router[:, my_cols]) for p in lg_parts)
-    combine(n - 1)
-    for c in (1, 2):
-        m_send[c - 1] = e_acc[c].astype(BF16)
-        far_copy(c).start()
-
     def gain_normed(r):
         cols = pl.ds(pl.multiple_of(r * kb, kb), kb)
         return 1.0 + scale[:, cols], (tokens[:, cols].astype(F32) - mean) * inv_std
@@ -485,6 +490,7 @@
     sums_t = jnp.where(lane == 0, sums[0], jnp.where(lane == 1, sums[1], 0.0)).T
     ns_own[...] = sums_t[:8]
     loop(1, zn, lambda j: ns_copy(j).start())
+    loop(last, nb, weight_grads)
 
     def finish(b):
         gu_copy(b).wait_recv()
@@ -528,7 +534,8 @@
 
     def drain_slot(k):
         sh_copy(k).wait_send()
-        b_copy(k).wait_send()
+        for c in range(3):
+            b_copy(k, c).wait_send()
         tb_copy(k).wait_send()
 
         @pl.when(k < RELAYED * n)
@@ -679,7 +686,7 @@
         vm((zn, 8, toks), F32),
     ]
     sems = [3, 3, 3, (slots, 3), (slots, 3), (n, 5), (n, 5), (n, 5), (n, 5)]
-    sems += [2, 2, slots, slots, slots, slots]
+    sems += [2, 2, (slots, 3), (slots, 3), slots, slots]
     sems += [zn, zn, slots, slots, nb, nb, nb, nb]
     sems += [1, 1, n, n, n, n, zn, zn]
     scratch += [dma(s if isinstance(s, tuple) else (s,)) for s in sems]

time: 114 us -> 106 us (0.930); the launches traced: 112 us -> 105 us
  Pallas kernels: 111 us -> 105 us
    pallas_call x1, Pallas kernels: 108 us -> 102 us  [shards(): pl.pallas_call(functools.partial(expert_kernel, n, zn), out_shape=(jax.Sh...]
where the time goes in v6:
time: 106 us; the launch traced here: 105 us
  Pallas kernels  105 us (99%)
    pallas_call x1, Pallas kernels, shards(): pl.pallas_call(functools.partial(expert_kernel, n, zn), out_shape=(jax.Sh...  102 us
    pallas_call x1, Pallas kernels, place_results(): pl.pallas_call(functools.partial(copy_kernel, count), out_shape=tuple((ja...  3.13 us

profile of v6, /device:TPU:32, one launch (start us, length us, event | category | flops | bytes accessed | tf_op | source)
XLA Modules:
  0.0 105.3 jit_solution(10362480380681277004)
XLA Ops:
  0.6 101.6 %shard_map.137 = (f32[128,512]{1,0:T(8,128)}, f32[16,512]{1,0:T(8,128)}, bf16[1,4096,128]{2,1,0:T(8,128)(2,1)}, bf16[1,4096,128]{2,1,0:T(8,128)(2,1)}, bf16[1,128,4096]{2,1,0:T(8,128)(2,1)}) custom-call(bf16[128,4096]{1,0:T(8,128)(2,1)} %refs_0_.1, bf16[128,4096]{1,0:T(8,128)(2,1)} %refs_1_.1, s32[2,128]{1,0:T(2,128)} %bitcast.11, f32[1,4096]{1,0:T(1,128)} %bitcast.8, ...), custom_call_target="tpu_custom_call" | custom-call | flops 6442450944 | bytes 16777216 | tf_op jit(solution)/shard_map/pallas_call | solution.py:696
  102.2 3.1 %shard_map.138 = (f32[128,512]{1,0:T(8,128)}, f32[16,512]{1,0:T(8,128)}, bf16[1,4096,128]{2,1,0:T(8,128)(2,1)}, bf16[1,4096,128]{2,1,0:T(8,128)(2,1)}, bf16[1,128,4096]{2,1,0:T(8,128)(2,1)}) custom-call(f32[128,512]{1,0:T(8,128)} %get-tuple-element.15.refs_0_, f32[16,512]{1,0:T(8,128)} %get-tuple-element.16.refs_1_, ...), custom_call_target="tpu_custom_call" | custom-call | tf_op jit(solution)/shard_map/pallas_call | solution.py:604

commit v7 on v6

--- a/solution.py
+++ b/solution.py
@@ -47,13 +47,13 @@
         (mod, og, place_t, send, recv, w_gate, w_up, w_down, rows_z, rows_wdy, d_gu, hid, hr),
         (gu_acc, r_acc, t_send, t_in, t_own, m_send, m_in, b_send, b_recv, e_acc),
         (term_own, term_z, term_sum, term_b, sh_own, sh_recv, sh_col),
-        (gu_own, gu_send, gu_recv, dn_own, dn_send, dn_recv),
+        (gu_own, gu_send, gu_recv, dn_own, dn_send, dn_recv, gate_st, up_st, down_st, out_sem),
         (logit_acc, stat, rc_own, rc_sib, rx_sum, rx_buf, ry_sum, ry_buf, ns_own, ns_z),
         (w_local, w_ssem, w_rsem, d_ssem, d_rsem, f_ssem, f_rsem, a_ssem, a_rsem),
         (m_ssem, m_rsem, b_ssem, b_rsem, sh_ssem, sh_rsem),
         (tz_ssem, tz_rsem, tb_ssem, tb_rsem, g_ssem, g_rsem, h_ssem, h_rsem),
         (rc_ssem, rc_rsem, rx_ssem, rx_rsem, ry_ssem, ry_rsem, ns_ssem, ns_rsem),
-    ) = split_refs(refs, (10, 5, 13, 10, 7, 6, 10, 9, 6, 8, 8))
+    ) = split_refs(refs, (10, 5, 13, 10, 7, 10, 10, 9, 6, 8, 8))
     slots = n * n
     width = rows_z.shape[1]
     group = n * CAP
@@ -271,7 +271,7 @@
                 if CLASS[i] == c:
                     relay_copy(g, i, own_class(c)).start()
 
-    relayed_start(0)
+    loop(0, RELAYED, relayed_start)
     logit_acc[...] = jnp.zeros_like(logit_acc)
 
     def add_logits(b):
@@ -293,7 +293,6 @@
     for i in range(nt):
         sh_own[i : i + 1, :] = share_row[:, 128 * i : 128 * (i + 1)]
     loop(1, slots, lambda k: sh_copy(k).start())
-    loop(1, RELAYED, relayed_start)
     loop(RELAYED, n, lambda g: loop(0, nb, lambda b: fill(g, b)))
     for g in range(RELAYED):
         relayed_arrive(g)
@@ -497,9 +496,9 @@
         dn_copy(b).wait_recv()
         cols = pl.ds(pl.multiple_of(b * kb, kb), kb)
         gu = gu_own[b] + gu_recv[b].astype(F32)
-        gate_out[0, cols, :] = gu[:, :hidden].astype(BF16)
-        up_out[0, cols, :] = gu[:, hidden:].astype(BF16)
-        down_out[0, :, cols] = (dn_own[b] + dn_recv[b].astype(F32)).astype(BF16)
+        gate_st[cols, :] = gu[:, :hidden].astype(BF16)
+        up_st[cols, :] = gu[:, hidden:].astype(BF16)
+        down_st[:, cols] = (dn_own[b] + dn_recv[b].astype(F32)).astype(BF16)
 
     rc_copy().wait_recv()
     rx_sum[...] = rc_own[...] + rc_sib[...]
@@ -514,6 +513,12 @@
     ry_buf[cy] = total
     loop(1, n, lambda j: ry_copy(j, cy).start())
     loop(nb // 2, nb, finish)
+    staged = ((gate_st, gate_out), (up_st, up_out), (down_st, down_out))
+    stores = [
+        pltpu.make_async_copy(src, dst.at[0], out_sem.at[i]) for i, (src, dst) in enumerate(staged)
+    ]
+    for store in stores:
+        store.start()
 
     for c in (1, 2):
         far_copy(c).wait_recv()
@@ -547,6 +552,8 @@
         def _():
             direct_copy(k).wait_send()
 
+    for store in stores:
+        store.wait()
     loop(1, slots, drain_slot)
 
     def drain_group(g):
@@ -674,6 +681,10 @@
         vm((nb, hidden, kb), F32),
         vm((nb, hidden, kb), BF16),
         vm((nb, hidden, kb), BF16),
+        vm((width, hidden), BF16),
+        vm((width, hidden), BF16),
+        vm((hidden, width), BF16),
+        dma((3,)),
         vm((toks, 128), F32),
         vm((toks, 128), F32),
         vm((16, cols_z), F32),
@@ -703,7 +714,7 @@
             jax.ShapeDtypeStruct((1, hidden, width), BF16),
         ),
         in_specs=[vm_spec] * 7 + [any_spec] * 3,
-        out_specs=(vm_spec,) * 5,
+        out_specs=(vm_spec,) * 2 + (any_spec,) * 3,
         scratch_shapes=scratch,
         compiler_params=pltpu.CompilerParams(
             collective_id=0, has_side_effects=True, vmem_limit_bytes=60 * 1024 * 1024

time: 106 us -> 104 us (0.981)
  Pallas kernels: 105 us -> 102 us
    pallas_call x1, Pallas kernels: 102 us -> 99.2 us  [shards(): pl.pallas_call(functools.partial(expert_kernel, n, zn), out_shape=(jax.Sh...]
where the time goes in v7:
time: 104 us; the launch traced here: 103 us
  Pallas kernels  102 us (98%)
    pallas_call x1, Pallas kernels, shards(): pl.pallas_call(functools.partial(expert_kernel, n, zn), out_shape=(jax.Sh...  99.2 us
    pallas_call x1, Pallas kernels, place_results(): pl.pallas_call(functools.partial(copy_kernel, count), out_shape=tuple((ja...  3.13 us

profile of v7, /device:TPU:32, one launch (start us, length us, event | category | flops | bytes accessed | tf_op | source)
XLA Modules:
  0.0 102.9 jit_solution(8311253755553792422)
XLA Ops:
  0.6 99.2 %shard_map.137 = (f32[128,512]{1,0:T(8,128)}, f32[16,512]{1,0:T(8,128)}, bf16[1,4096,128]{2,1,0:T(8,128)(2,1)}, bf16[1,4096,128]{2,1,0:T(8,128)(2,1)}, bf16[1,128,4096]{2,1,0:T(8,128)(2,1)}) custom-call(bf16[128,4096]{1,0:T(8,128)(2,1)} %refs_0_.1, bf16[128,4096]{1,0:T(8,128)(2,1)} %refs_1_.1, s32[2,128]{1,0:T(2,128)} %bitcast.11, f32[1,4096]{1,0:T(1,128)} %bitcast.8, ...), custom_call_target="tpu_custom_call" | custom-call | flops 6442450944 | bytes 16777216 | tf_op jit(solution)/shard_map/pallas_call | solution.py:707
  99.8 3.1 %shard_map.138 = (f32[128,512]{1,0:T(8,128)}, f32[16,512]{1,0:T(8,128)}, bf16[1,4096,128]{2,1,0:T(8,128)(2,1)}, bf16[1,4096,128]{2,1,0:T(8,128)(2,1)}, bf16[1,128,4096]{2,1,0:T(8,128)(2,1)}) custom-call(f32[128,512]{1,0:T(8,128)} %get-tuple-element.15.refs_0_, f32[16,512]{1,0:T(8,128)} %get-tuple-element.16.refs_1_, ...), custom_call_target="tpu_custom_call" | custom-call | tf_op jit(solution)/shard_map/pallas_call | solution.py:611

commit v8 on v7

--- a/solution.py
+++ b/solution.py
@@ -10,6 +10,7 @@
 
 CAP = 24
 RELAYED = 3
+PARTS = 4
 ROLE = (1, 7, 4, 2, 5)
 CLASS = (0, 0, 1, 1, 2)
 SIGN = (1, -1, 1, -1, -1)
@@ -592,15 +593,25 @@
 def copy_kernel(count, *refs):
     sems = refs[-1]
     held = refs[2 * count : 3 * count]
-    arrive = [pltpu.make_async_copy(refs[i], held[i], sems.at[0, i]) for i in range(count)]
+    pieces = []
+    for i in range(count):
+        cuts = PARTS if len(held[i].shape) == 3 else 1
+        step = held[i].shape[-2] // cuts
+        for part in range(cuts):
+            rows = pl.ds(part * step, step)
+            at = (0, rows) if len(held[i].shape) == 3 else (rows,)
+            pieces.append((refs[i].at[at], held[i].at[at], refs[count + i].at[at]))
+    arrive = [
+        pltpu.make_async_copy(src, mid, sems.at[0, p]) for p, (src, mid, dst) in enumerate(pieces)
+    ]
     leave = [
-        pltpu.make_async_copy(held[i], refs[count + i], sems.at[1, i]) for i in range(count)
+        pltpu.make_async_copy(mid, dst, sems.at[1, p]) for p, (src, mid, dst) in enumerate(pieces)
     ]
     for copy in arrive:
         copy.start()
-    for i in range(count):
-        arrive[i].wait()
-        leave[i].start()
+    for p in range(len(pieces)):
+        arrive[p].wait()
+        leave[p].start()
     for copy in leave:
         copy.wait()
 
@@ -614,7 +625,7 @@
         in_specs=[any_spec] * count,
         out_specs=(any_spec,) * count,
         scratch_shapes=[pltpu.VMEM(a.shape, a.dtype) for a in arrays]
-        + [pltpu.SemaphoreType.DMA((2, count))],
+        + [pltpu.SemaphoreType.DMA((2, PARTS * count))],
         compiler_params=pltpu.CompilerParams(vmem_limit_bytes=60 * 1024 * 1024),
     )(*arrays)
 

time: 104 us -> 104 us (level)
  no operation moved by 1% of the time
where the time goes in v8:
time: 104 us; the launch traced here: 103 us
  Pallas kernels  102 us (98%)
    pallas_call x1, Pallas kernels, shards(): pl.pallas_call(functools.partial(expert_kernel, n, zn), out_shape=(jax.Sh...  99.2 us
    pallas_call x1, Pallas kernels, place_results(): pl.pallas_call(functools.partial(copy_kernel, count), out_shape=tuple((ja...  3.14 us

profile of v8, /device:TPU:32, one launch (start us, length us, event | category | flops | bytes accessed | tf_op | source)
XLA Modules:
  0.0 102.9 jit_solution(17637875639039281536)
XLA Ops:
  0.6 99.2 %shard_map.137 = (f32[128,512]{1,0:T(8,128)}, f32[16,512]{1,0:T(8,128)}, bf16[1,4096,128]{2,1,0:T(8,128)(2,1)}, bf16[1,4096,128]{2,1,0:T(8,128)(2,1)}, bf16[1,128,4096]{2,1,0:T(8,128)(2,1)}) custom-call(bf16[128,4096]{1,0:T(8,128)(2,1)} %refs_0_.1, bf16[128,4096]{1,0:T(8,128)(2,1)} %refs_1_.1, s32[2,128]{1,0:T(2,128)} %bitcast.11, f32[1,4096]{1,0:T(1,128)} %bitcast.8, ...), custom_call_target="tpu_custom_call" | custom-call | flops 6442450944 | bytes 16777216 | tf_op jit(solution)/shard_map/pallas_call | solution.py:718
  99.8 3.1 %shard_map.138 = (f32[128,512]{1,0:T(8,128)}, f32[16,512]{1,0:T(8,128)}, bf16[1,4096,128]{2,1,0:T(8,128)(2,1)}, bf16[1,4096,128]{2,1,0:T(8,128)(2,1)}, bf16[1,128,4096]{2,1,0:T(8,128)(2,1)}) custom-call(f32[128,512]{1,0:T(8,128)} %get-tuple-element.15.refs_0_, f32[16,512]{1,0:T(8,128)} %get-tuple-element.16.refs_1_, ...), custom_call_target="tpu_custom_call" | custom-call | tf_op jit(solution)/shard_map/pallas_call | solution.py:622
